TPU v7x, 128 devices: a whole 4x4x4 slice. The times are simulated.
128 devices in a mesh: bal: 16 (over z, x), grp: 8 (over y, core).
Axes of the slice: x: 4, y: 4, z: 4, core: 2. Of those that a mesh axis runs over, the one named last changes fastest.
Arguments:
- table: bfloat16 [262144, 512], P(('bal', 'grp')), may hold values from -6 to 6
- item_owner: int32 [8, 4096, 1], P('grp', 'bal'), may hold values from 0 to 127; in each aligned block of 256 rows (0 to 255, 256 to 511, ..., all dimensions but the last counted through in order) at most 8 rows name the same one
- item_row: int32 [8, 4096], P('grp', 'bal'), may hold values from 0 to 2047
- segment: int32 [8, 4096], P('grp', 'bal'), may hold values from 0 to 7, never falling along the last dimension, each value on 1 to 2048 neighbouring positions
- w_in: bfloat16 [512, 1024], replicated, may hold values from -0.25 to 0.25
- w_out: bfloat16 [256, 512], replicated, may hold values from -0.375 to 0.375
- cotangent: bfloat16 [8, 4096, 512], P('grp', 'bal'), may hold values from -6 to 6
Outputs:
- layer_out: bfloat16 [8, 4096, 512], P('grp', 'bal')
- table_grad: float32 [262144, 512], P(('bal', 'grp'))
- w_in_grad: float32 [512, 1024], replicated
- w_out_grad: float32 [256, 512], replicated
Inputs may be any that keep to these rules, and one draw needn't show every extreme that they name: `item_owner`: of the actions of one device at most 8 name the same row block, and in some device exactly 8 do. `segment`: along each group's actions the history number never falls; each history holds 1 to 2048 actions and one holds exactly 2048.
All inputs are finite; a program needn't handle non-finite values.
Results may differ from a plain program's by a relative error of at most 0.0091.
Values may be sent and summed in bfloat16 or wider, within the bound.
A program may use at most 128 MiB of HBM per device.

v0:
```python
import jax
import jax.numpy as jnp
from jax import lax
from jax.sharding import PartitionSpec as P

HEADS = 4
DH = 64


norm_eps = 1e-06
contract_rows = (((0,), (0,)), ((), ()))
contract_cols = (((1,), (1,)), ((), ()))


def layer_norm(values):
    average = jnp.mean(values, axis=-1, keepdims=True)
    centred = values - average
    spread = jnp.mean(centred * centred, axis=-1, keepdims=True)
    return centred * lax.rsqrt(spread + norm_eps)


def output_norm(attended, gate):
    return layer_norm(attended) * gate


def silu_slope(values):
    sigmoids = jax.nn.sigmoid(values)
    return sigmoids * (1.0 + values * (1.0 - sigmoids))


def by_heads(values):
    return values.reshape(values.shape[0], HEADS, DH)


def visible_pairs(query_pos, query_seg, key_pos, key_seg):
    return (query_seg[:, None] == key_seg[None, :]) & (key_pos[None, :] <= query_pos[:, None])


def pair_terms(queries, keys_in, visible, len_max):
    scores = jnp.einsum("qhd,khd->hqk", queries, keys_in, preferred_element_type=jnp.float32)
    sigmoids = jax.nn.sigmoid(scores)
    weight = jnp.where(visible[None], scores * sigmoids / len_max, 0.0)
    slopes = jnp.where(visible[None], sigmoids * (1.0 + scores * (1.0 - sigmoids)) / len_max, 0.0)
    return (weight, slopes)


def sweep(block_step, carry, amount):
    block = amount
    while block > 1024 and block % 2 == 0:
        block = block // 2
    return lax.fori_loop(
        0,
        amount // block,
        lambda counter, current: block_step(current, counter * block, block),
        carry,
    )


def send_requests(buffer):
    return lax.all_to_all(buffer, ("bal", "grp"), split_axis=0, concat_axis=0, tiled=True)


def send_rows(buffer):
    return lax.all_to_all(buffer, ("bal", "grp"), split_axis=0, concat_axis=0, tiled=True)


def send_grads(buffer):
    return lax.all_to_all(buffer, ("bal", "grp"), split_axis=0, concat_axis=0, tiled=True)


def per_device(table, item_owner, item_row, segment, w_in, w_out, cotangent):
    n_bal = lax.axis_size("bal")
    n_grp = lax.axis_size("grp")
    devices = n_bal * n_grp
    owners = item_owner[0, :, 0]
    rows_here = item_row[0]
    segments = segment[0]
    upstream = cotangent[0]
    actions = rows_here.shape[0]
    width = table.shape[1]
    hidden = w_out.shape[0]
    group_len = actions * n_bal
    len_max = group_len // 2
    capacity = max(4, 4 * actions // devices)
    owner_hot = (owners[:, None] == jnp.arange(devices, dtype=jnp.int32)[None, :]).astype(jnp.int32)
    earlier = jnp.cumsum(owner_hot, axis=0) - owner_hot
    ranks = jnp.sum(earlier * owner_hot, axis=1)
    slots = owners * capacity + ranks
    requests = jnp.zeros((devices * capacity,), jnp.int32).at[slots].set(rows_here)
    wanted = send_requests(requests.reshape(devices, capacity)).reshape(-1)
    fetched = table[wanted].reshape(devices, capacity, width)
    arrived = send_rows(fetched).reshape(devices * capacity, width)
    embedded = arrived[slots]
    normed = layer_norm(embedded.astype(jnp.float32)).astype(jnp.bfloat16)
    pre_act = jnp.dot(normed, w_in, preferred_element_type=jnp.float32)
    activated = jax.nn.silu(pre_act)
    gate = activated[:, :hidden].astype(jnp.bfloat16)
    value_rows = activated[:, hidden : 2 * hidden].astype(jnp.bfloat16)
    query_rows = activated[:, 2 * hidden : 3 * hidden].astype(jnp.bfloat16)
    key_rows = activated[:, 3 * hidden :].astype(jnp.bfloat16)
    all_segments = lax.all_gather(segments, "bal", axis=0, tiled=True)
    my_pos = lax.axis_index("bal") * actions + jnp.arange(actions, dtype=jnp.int32)
    query_heads = by_heads(query_rows)
    head_zeros = jnp.zeros((actions, HEADS, DH), jnp.float32)
    key_part = lax.all_gather(key_rows, "bal", axis=0, tiled=True)
    value_part = lax.all_gather(value_rows, "bal", axis=0, tiled=True)

    def block_step(running, offset, amount):
        key_block = by_heads(lax.dynamic_slice_in_dim(key_part, offset, amount, 0))
        value_block = by_heads(lax.dynamic_slice_in_dim(value_part, offset, amount, 0))
        key_pos = offset + jnp.arange(amount, dtype=jnp.int32)
        key_seg = lax.dynamic_slice_in_dim(all_segments, offset, amount, 0)
        weight, _ = pair_terms(
            query_heads, key_block, visible_pairs(my_pos, segments, key_pos, key_seg), len_max
        )
        return running + jnp.einsum(
            "hqk,khd->qhd",
            weight.astype(jnp.bfloat16),
            value_block,
            preferred_element_type=jnp.float32,
        )

    attended = sweep(block_step, head_zeros, key_part.shape[0]).reshape(actions, hidden)
    mixed, post_back = jax.vjp(output_norm, attended, gate.astype(jnp.float32))
    mixed_low = mixed.astype(jnp.bfloat16)
    layer_out = (
        jnp.dot(mixed_low, w_out, preferred_element_type=jnp.float32) + embedded.astype(jnp.float32)
    ).astype(jnp.bfloat16)
    w_out_part = lax.dot_general(
        mixed_low, upstream, contract_rows, preferred_element_type=jnp.float32
    )
    d_mixed = lax.dot_general(upstream, w_out, contract_cols, preferred_element_type=jnp.float32)
    d_attended, d_gate = post_back(d_mixed)
    deltas = d_attended.astype(jnp.bfloat16)
    gate_grad = d_gate.astype(jnp.bfloat16)
    delta_heads = by_heads(deltas)
    group_zeros = jnp.zeros((group_len, hidden), jnp.float32)
    joint_key_part = lax.all_gather(key_rows, "bal", axis=0, tiled=True)
    joint_value_part = lax.all_gather(value_rows, "bal", axis=0, tiled=True)

    def block_step(running, offset, amount):
        query_total, key_terms, value_terms = running
        key_block = by_heads(lax.dynamic_slice_in_dim(joint_key_part, offset, amount, 0))
        value_block = by_heads(lax.dynamic_slice_in_dim(joint_value_part, offset, amount, 0))
        key_pos = offset + jnp.arange(amount, dtype=jnp.int32)
        key_seg = lax.dynamic_slice_in_dim(all_segments, offset, amount, 0)
        weight, slopes = pair_terms(
            query_heads, key_block, visible_pairs(my_pos, segments, key_pos, key_seg), len_max
        )
        product = jnp.einsum(
            "qhd,khd->hqk", delta_heads, value_block, preferred_element_type=jnp.float32
        )
        d_score = (product * slopes).astype(jnp.bfloat16)
        query_total = query_total + jnp.einsum(
            "hqk,khd->qhd", d_score, key_block, preferred_element_type=jnp.float32
        )
        key_piece_grad = jnp.einsum(
            "hqk,qhd->khd", d_score, query_heads, preferred_element_type=jnp.float32
        )
        value_piece_grad = jnp.einsum(
            "hqk,qhd->khd",
            weight.astype(jnp.bfloat16),
            delta_heads,
            preferred_element_type=jnp.float32,
        )
        key_terms = lax.dynamic_update_slice_in_dim(
            key_terms, key_piece_grad.reshape(amount, hidden), offset, 0
        )
        value_terms = lax.dynamic_update_slice_in_dim(
            value_terms, value_piece_grad.reshape(amount, hidden), offset, 0
        )
        return (query_total, key_terms, value_terms)

    query_grad, key_terms, value_terms = sweep(
        block_step, (head_zeros, group_zeros, group_zeros), joint_key_part.shape[0]
    )
    key_grad, value_grad = (
        lax.psum_scatter(key_terms, "bal", scatter_dimension=0, tiled=True),
        lax.psum_scatter(value_terms, "bal", scatter_dimension=0, tiled=True),
    )
    joined = jnp.concatenate(
        [
            gate_grad,
            value_grad.astype(jnp.bfloat16),
            query_grad.reshape(actions, hidden).astype(jnp.bfloat16),
            key_grad.astype(jnp.bfloat16),
        ],
        axis=1,
    )
    d_pre = (joined.astype(jnp.float32) * silu_slope(pre_act)).astype(jnp.bfloat16)
    w_in_part = lax.dot_general(normed, d_pre, contract_rows, preferred_element_type=jnp.float32)
    d_normed = lax.dot_general(d_pre, w_in, contract_cols, preferred_element_type=jnp.float32)
    _, norm_back = jax.vjp(layer_norm, embedded.astype(jnp.float32))
    d_embedded = norm_back(d_normed)[0] + upstream.astype(jnp.float32)
    outgoing = jnp.zeros((devices * capacity, width), jnp.float32).at[slots].set(d_embedded)
    landed = send_grads(outgoing.reshape(devices, capacity, width)).reshape(
        devices * capacity, width
    )
    table_grad = jnp.zeros((table.shape[0], width), jnp.float32).at[wanted].add(landed)
    w_in_grad, w_out_grad = lax.psum((w_in_part, w_out_part), ("bal", "grp"))
    return (layer_out[None], table_grad, w_in_grad, w_out_grad)


def solution(mesh):
    placed = (
        P(("bal", "grp"), None),
        P("grp", "bal", None),
        P("grp", "bal"),
        P("grp", "bal"),
        P(),
        P(),
        P("grp", "bal", None),
    )
    return jax.shard_map(
        per_device,
        mesh=mesh,
        in_specs=placed,
        out_specs=(P("grp", "bal", None), P(("bal", "grp"), None), P(), P()),
        check_vma=False,
    )
```

profile of v0, /device:TPU:1, one launch (start us, length us, event | category | flops | bytes accessed | tf_op | source)
XLA Modules:
  0.0 648.5 jit_solution(549367521040187435)
XLA Ops:
  11.6 20.9 %all_to_all.19 = s32[128,1,8]{2,1,0:T(1,128)S(1)} all-to-all(s32[128,1,8]{2,1,0:T(1,128)S(1)} %bitcast.213), channel_id=1, replica_groups=mesh['bal'=16,'grp'=8] {'bal','grp'}, dimensions={0} | all-to-all | bytes 8192 | tf_op jit(solution)/shard_map/all_to_all | solution.py:60
  34.6 5.1 gather_fusion
  39.6 4.4 all-to-all-start.1
  44.1 18.8 %all-to-all-done.1 = bf16[128,8,512]{2,1,0:T(8,128)(2,1)S(1)} async-done(((bf16[128,8,512]{2,1,0:T(8,128)(2,1)}), bf16[128,8,512]{2,1,0:T(8,128)(2,1)S(1)}, u32[]{:S(2)}, u32[]{:S(2)}) %all-to-all-start.1) | async-done | bytes 1048608 | tf_op jit(solution)/shard_map/all_to_all | solution.py:64
  70.2 16.9 %all-gather = s32[1,4096]{1,0:T(1,128)S(1)} all-gather(s32[1,256]{1,0:T(1,128)S(1)} %copy-done.11), channel_id=2, replica_groups=mesh['bal'=16,'grp'=8] {'bal'}, dimensions={1}, use_global_device_ids=true | all-gather | bytes 17408 | tf_op jit(solution)/shard_map/all_gather | solution.py:101
  87.2 22.9 %all-gather.4.cloned.1.call-done = bf16[4096,256]{1,0:T(8,128)(2,1)} async-done(((bf16[256,256]{1,0:T(8,128)(2,1)}), bf16[4096,256]{1,0:T(8,128)(2,1)}) %all-gather.4.cloned.1.call-update) | async-done | bytes 2097168 | tf_op jit(solution)/shard_map/all_gather | solution.py:106
  110.0 4.1 copy.55
  114.1 43.2 %all-gather.6.cloned.1.call-done = bf16[4096,256]{1,0:T(8,128)(2,1)} async-done(((bf16[256,256]{1,0:T(8,128)(2,1)}), bf16[4096,256]{1,0:T(8,128)(2,1)}) %all-gather.6.cloned.1.call-update) | async-done | bytes 2097168 | tf_op jit(solution)/shard_map/all_gather | solution.py:105
  157.3 4.1 copy.56
  161.4 26.0 %while.32 = (s32[]{:T(128)}, f32[256,4,64]{0,2,1:T(8,128)}, bf16[4096,256]{0,1:T(8,128)(2,1)}, s32[1,256]{1,0:T(1,128)}, s32[4096]{0:T(1024)S(1)}, /*index=5*/bf...) while((s32[]{:T(128)}, f32[256,4,64]{0,2,1:T(8,128)}, ...), condition=%wide.region_7.8_spmd.clone, body=%wide.region_6.7_spmd.clone.sunk | while | flops 276694272 | bytes 4349125 | solution.py:51
  164.5 3.4 fusion.118
  170.9 3.5 fusion.118
  177.4 3.5 fusion.118
  183.9 3.5 fusion.118
  199.2 98.7 %while.33 = (s32[]{:T(128)}, f32[256,4,64]{0,2,1:T(8,128)}, f32[4096,256]{1,0:T(8,128)}, f32[4096,256]{1,0:T(8,128)}, bf16[4096,256]{0,1:T(8,128)(2,1)}, /*index...) while((s32[]{:T(128)}, f32[256,4,64]{0,2,1:T(8,128)}, ...), condition=%wide.region_13.14_spmd.clone, body=%wide.region_12.13_spmd.clone.sunk | while | flops 690881792 | bytes 53243220 | solution.py:51
  203.0 3.4 fusion.130
  209.2 4.6 fusion.132
  227.6 3.4 fusion.130
  233.8 4.6 fusion.132
  240.0 3.3 fusion.133
  252.3 3.4 fusion.130
  258.5 4.6 fusion.132
  277.0 3.4 fusion.130
  283.2 4.6 fusion.132
  289.3 3.3 fusion.133
  298.9 75.6 %reduce-scatter.5.cloned.1.call-done = f32[256,256]{1,0:T(8,128)} async-done(((f32[4096,256]{1,0:T(8,128)}), f32[256,256]{1,0:T(8,128)}) %reduce-scatter.5.cloned.1.call-update) | async-done | bytes 262160 | tf_op jit(solution)/shard_map/reduce_scatter | solution.py:178
  375.5 79.7 %reduce-scatter.3.cloned.1.call-done = f32[256,256]{1,0:T(8,128)} async-done(((f32[4096,256]{1,0:T(8,128)}), f32[256,256]{1,0:T(8,128)}) %reduce-scatter.3.cloned.1.call-update) | async-done | bytes 262160 | tf_op jit(solution)/shard_map/reduce_scatter | solution.py:179
  459.9 3.5 scatter_custom_fusion.1
  463.4 9.6 %all-to-all-start.2 = ((f32[128,8,512]{2,1,0:T(8,128)}), f32[128,8,512]{2,1,0:T(8,128)}, u32[]{:S(2)}, u32[]{:S(2)}) async-start(f32[128,8,512]{2,1,0:T(8,128)} %bitcast.207), calls=%async_computation.4 | async-start | bytes 4194304 | tf_op jit(solution)/shard_map/all_to_all | solution.py:68
  477.0 26.5 %all-to-all-done.2 = f32[128,8,512]{2,1,0:T(8,128)} async-done(((f32[128,8,512]{2,1,0:T(8,128)}), f32[128,8,512]{2,1,0:T(8,128)}, u32[]{:S(2)}, u32[]{:S(2)}) %all-to-all-start.2) | async-done | bytes 2097184 | tf_op jit(solution)/shard_map/all_to_all | solution.py:68
  503.5 9.6 %scatter_custom_fusion.2 = f32[2048,512]{1,0:T(8,128)} fusion(s32[1024]{0:T(1024)} %bitcast.220, f32[128,8,512]{2,1,0:T(8,128)} %all-to-all-done.2, f32[]{:T(128)} %constant.133.clone.1), kind=kCustom, calls=%fused_computation.54 | custom fusion | flops 524288 | bytes 6291968 | tf_op jit(solution)/shard_map/scatter-add | solution.py:199
  513.1 124.8 %all-reduce.3.cloned.1.call-done = (f32[512,1024]{1,0:T(8,128)}, f32[256,512]{1,0:T(8,128)}) async-done(((f32[512,1024]{1,0:T(8,128)}, f32[256,512]{1,0:T(8,128)}), (f32[512,1024]{1,0:T(8,128)}, f32[256,512]{1,0:T(8,128)})) %all-reduce.3.cloned.1.call-update) | async-done | bytes 2621456 | tf_op jit(solution)/shard_map/psum | solution.py:200
  (196 shorter events, 111.8 us)
Async XLA Ops:
  7.2 27.4 %copy-start = (bf16[2048,512]{1,0:T(8,128)(2,1)S(1)}, bf16[2048,512]{1,0:T(8,128)(2,1)}, u32[]{:S(2)}) copy-start(bf16[2048,512]{1,0:T(8,128)(2,1)} %param.11) | copy-start | bytes 6291460
  10.0 34.1 %copy-start.20 = (s32[256,1]{0,1:T(1,128)}, s32[256,1]{0,1:T(1,128)S(1)}, u32[]{:S(2)}) copy-start(s32[256,1]{0,1:T(1,128)S(1)} %compare_select_fusion.1) | copy-start | bytes 3076
  39.6 23.3 %all-to-all-start.1 = ((bf16[128,8,512]{2,1,0:T(8,128)(2,1)}), bf16[128,8,512]{2,1,0:T(8,128)(2,1)S(1)}, u32[]{:S(2)}, u32[]{:S(2)}) async-start(bf16[128,8,512]{2,1,0:T(8,128)(2,1)} %bitcast.208), calls=%async_computation.1 | async-start | bytes 2097152 | tf_op jit(solution)/shard_map/all_to_all | solution.py:64
  44.0 66.0 %all-gather.4.cloned.1.call-start = ((), (), s32[]{:S(2)}) async-start(), calls=%async_computation.5 | async-start | bytes 2228224 | tf_op jit(solution)/shard_map/all_gather | solution.py:106
  64.1 6.1 copy-start.11
  64.2 5.1 copy-start.13
  65.1 4.3 copy-start.15
  69.4 87.9 %all-gather.6.cloned.1.call-start = ((), (), s32[]{:S(2)}) async-start(), calls=%async_computation.6 | async-start | bytes 2228224 | tf_op jit(solution)/shard_map/all_gather | solution.py:105
  70.1 304.4 %reduce-scatter.5.cloned.1.call-start = ((), (), s32[]{:S(2)}) async-start(), calls=%async_computation.8 | async-start | bytes 4456448 | tf_op jit(solution)/shard_map/reduce_scatter | solution.py:178
  199.2 3.8 copy-start.10
  201.0 5.3 copy-start.1
  203.0 3.4 copy-start.3
  223.8 3.4 copy-start.12
  223.8 3.8 copy-start.10
  225.7 5.3 copy-start.1
  227.6 3.4 copy-start.3
  248.5 3.8 copy-start.10
  250.4 5.3 copy-start.1
  252.3 3.4 copy-start.3
  273.2 3.4 copy-start.12
  273.2 3.8 copy-start.10
  275.1 5.3 copy-start.1
  277.0 3.4 copy-start.3
  297.9 158.3 %copy-start.8 = (bf16[256,256]{1,0:T(8,128)(2,1)S(1)}, bf16[256,256]{1,0:T(8,128)(2,1)}, u32[]{:S(2)}) copy-start(bf16[256,256]{1,0:T(8,128)(2,1)} %get-tuple-element.506) | copy-start | bytes 393220
  297.9 159.9 %copy-start.14 = (f32[256]{0:T(256)S(1)}, f32[256]{0:T(256)}, u32[]{:S(2)}) copy-start(f32[256]{0:T(256)} %copy-done.13) | copy-start | bytes 3076
  297.9 157.3 %reduce-scatter.3.cloned.1.call-start = ((), (), s32[]{:S(2)}) async-start(), calls=%async_computation.7 | async-start | bytes 4456448 | tf_op jit(solution)/shard_map/reduce_scatter | solution.py:179
  298.2 161.4 %copy-start.19 = (f32[256]{0:T(256)S(1)}, f32[256]{0:T(256)}, u32[]{:S(2)}) copy-start(f32[256]{0:T(256)} %copy-done.18) | copy-start | bytes 3076
  298.2 161.4 %copy-start.16 = (f32[256]{0:T(256)S(1)}, f32[256]{0:T(256)}, u32[]{:S(2)}) copy-start(f32[256]{0:T(256)} %copy-done.15) | copy-start | bytes 3076
  459.6 13.5 %copy-start.5 = (bf16[256,256]{1,0:T(8,128)(2,1)S(1)}, bf16[256,256]{1,0:T(8,128)(2,1)}, u32[]{:S(2)}) copy-start(bf16[256,256]{1,0:T(8,128)(2,1)} %get-tuple-element.505) | copy-start | bytes 393220
  463.4 9.7 %copy-start.4 = (bf16[1,256,512]{2,1,0:T(8,128)(2,1)S(1)}, bf16[1,256,512]{2,1,0:T(8,128)(2,1)}, u32[]{:S(2)}) copy-start(bf16[1,256,512]{2,1,0:T(8,128)(2,1)} %param.17) | copy-start | bytes 786436
  463.4 40.1 %all-to-all-start.2 = ((f32[128,8,512]{2,1,0:T(8,128)}), f32[128,8,512]{2,1,0:T(8,128)}, u32[]{:S(2)}, u32[]{:S(2)}) async-start(f32[128,8,512]{2,1,0:T(8,128)} %bitcast.207), calls=%async_computation.4 | async-start | bytes 4194304 | tf_op jit(solution)/shard_map/all_to_all | solution.py:68
  473.0 164.9 %all-reduce.3.cloned.1.call-start = ((), (), s32[]{:S(2)}) async-start(), calls=%async_computation.9 | async-start | bytes 5242880 | tf_op jit(solution)/shard_map/psum | solution.py:200
  (8 other events, 16.1 us)
Sparse Core Ops, SparseCore 0:
  69.5 40.4 all-gather.3
  112.8 44.5 all-gather.5
  298.0 76.4 reduce-scatter.4
  378.1 77.0 reduce-scatter.2
  479.1 158.7 all-reduce.2
where the time goes:
time: 651 us; the launch traced here: 648 us
  waiting for transfers between devices  392 us (60%)
  matrix products  83.1 us (13%)
  local copies, waits for them, and re-layouts  73.9 us (11%)
  blocking collectives  37.8 us (6%)
  other arithmetic  32.2 us (5%)
  starting transfers between devices  14.4 us (2%)
  between operations  14.1 us (2%)
    psum x1, waiting for transfers between devices, per_device(): w_in_grad, w_out_grad = lax.psum((w_in_part, w_out_part), ('bal', 'grp'))  125 us
    reduce_scatter x1, waiting for transfers between devices, per_device(): lax.psum_scatter(value_terms, 'bal', scatter_dimension=0, tiled=True)  79.7 us
    reduce_scatter x1, waiting for transfers between devices, per_device(): lax.psum_scatter(key_terms, 'bal', scatter_dimension=0, tiled=True)  75.6 us
    all_gather x1, waiting for transfers between devices, per_device(): key_part = lax.all_gather(key_rows, 'bal', axis=0, tiled=True)  43.2 us
    all_to_all x1, waiting for transfers between devices, send_grads(): lax.all_to_all(buffer, ('bal', 'grp'), split_axis=0, concat_axis=0, tiled...  26.5 us
    all_gather x1, waiting for transfers between devices, per_device(): value_part = lax.all_gather(value_rows, 'bal', axis=0, tiled=True)  22.9 us
    all_to_all x1, blocking collectives, send_requests(): lax.all_to_all(buffer, ('bal', 'grp'), split_axis=0, concat_axis=0, tiled...  20.9 us
    all_to_all x1, waiting for transfers between devices, send_rows(): lax.all_to_all(buffer, ('bal', 'grp'), split_axis=0, concat_axis=0, tiled...  18.8 us
  transfers between devices with their start and end apart: 7, of which 7 were waited for; matrix products, arithmetic and copies ran while one was open for 3% of the time, Pallas kernels for 0%

commit v1 on v0

--- a/solution.py
+++ b/solution.py
@@ -1,6 +1,8 @@
 import jax
 import jax.numpy as jnp
 from jax import lax
+from jax.experimental import pallas as pl
+from jax.experimental.pallas import tpu as pltpu
 from jax.sharding import PartitionSpec as P
 
 HEADS = 4
@@ -56,41 +58,313 @@
     )
 
 
-def send_requests(buffer):
-    return lax.all_to_all(buffer, ("bal", "grp"), split_axis=0, concat_axis=0, tiled=True)
-
-
-def send_rows(buffer):
-    return lax.all_to_all(buffer, ("bal", "grp"), split_axis=0, concat_axis=0, tiled=True)
-
-
-def send_grads(buffer):
-    return lax.all_to_all(buffer, ("bal", "grp"), split_axis=0, concat_axis=0, tiled=True)
+MESH = pl.DeviceIdType.MESH
+BF = jnp.bfloat16
+F32 = jnp.float32
+TOK = 256
+WIDTH = 512
+CAP = 8
+ROWS = 2048
+NB = 16
+NG = 8
+DEV = NB * NG
+SLOTS = DEV * CAP
+
+
+def iota(shape, dim):
+    return lax.broadcasted_iota(jnp.int32, shape, dim)
+
+
+def hot(mask):
+    return jnp.where(mask, 1.0, 0.0).astype(BF)
+
+
+def dot(a, b):
+    return jnp.dot(a, b, preferred_element_type=F32)
+
+
+def dot_t(a, b):
+    return lax.dot_general(a, b, (((1,), (1,)), ((), ())), preferred_element_type=F32)
+
+
+def column_of(line):
+    size = line.shape[1]
+    eye = iota((size, size), 0) == iota((size, size), 1)
+    return jnp.sum(jnp.where(eye, line, 0.0), axis=1, keepdims=True)
+
+
+def line_of(column):
+    size = column.shape[0]
+    eye = iota((size, size), 0) == iota((size, size), 1)
+    return jnp.sum(jnp.where(eye, column, 0.0), axis=0, keepdims=True)
+
+
+def device(p):
+    return (p // NG, lax.rem(p, NG))
+
+
+def greet_all(me):
+    barrier = pltpu.get_barrier_semaphore()
+
+    def greet(k, carry):
+        pl.semaphore_signal(
+            barrier, inc=1, device_id=device(lax.rem(me + k, DEV)), device_id_type=MESH
+        )
+        return carry
+
+    lax.fori_loop(1, DEV, greet, 0)
+    return barrier
+
+
+def paired_halves(rows):
+    count = rows.shape[0] // CAP
+    split = rows.reshape(count, CAP, WIDTH)
+    joined = jnp.concatenate([split[:, :, : WIDTH // 2], split[:, :, WIDTH // 2 :]], axis=1)
+    return joined.reshape(count * 2 * CAP, WIDTH // 2).astype(BF)
+
+
+def wait_bytes(view, sem):
+    pltpu.make_async_copy(view, view, sem).wait()
+
+
+def fetch_kernel(
+    owner_ref, row_ref, seg_ref, table_hbm,
+    emb_ref, want_ref, slot_ref, start_ref,
+    table_v, asked, asks, want_v, rows_out, rows_in, count_out, count_in,
+    sems, count_send, count_recv,
+):
+    b, g = lax.axis_index("bal"), lax.axis_index("grp")
+    me = b * NG + g
+    barrier = greet_all(me)
+    load = pltpu.make_async_copy(table_hbm, table_v, sems.at[0])
+    load.start()
+    owner = owner_ref[...]
+    owner_f = owner.astype(F32)
+    lanes = iota((TOK, 128), 1)
+    named = jnp.where(owner == lanes, 1.0, 0.0)
+    before = hot(iota((TOK, TOK), 0) > iota((TOK, TOK), 1))
+    rank = jnp.sum(dot(before, named.astype(BF)) * named, axis=1, keepdims=True)
+    slot = owner_f * CAP + rank
+    slot_ref[...] = jnp.broadcast_to(line_of(slot), (8, TOK)).astype(jnp.int32)
+    ask = column_of(row_ref[...].astype(F32)) + 1.0
+    high = jnp.floor(ask * (1.0 / 64.0))
+    low = ask - 64.0 * high
+    mine = rank.astype(jnp.int32) == lanes // 16
+    named_t = hot(line_of(owner_f).astype(jnp.int32) == iota((DEV, TOK), 0))
+    asked[...] = (
+        64.0 * dot(named_t, jnp.where(mine, high, 0.0).astype(BF))
+        + dot(named_t, jnp.where(mine, low, 0.0).astype(BF))
+    ).astype(jnp.int32).reshape(DEV, 1, 128)
+    seg = column_of(seg_ref[...].astype(F32)).astype(jnp.int32)
+    below = jnp.sum(jnp.where(seg < lanes, 1.0, 0.0), axis=0, keepdims=True)
+    count_out[...] = jnp.broadcast_to(below, (8, 128))
+    count_in[b] = jnp.broadcast_to(below, (8, 128))
+    own = pltpu.make_async_copy(asked.at[me], asks.at[me], sems.at[1])
+    own.start()
+    own.wait()
+    pl.semaphore_wait(barrier, DEV - 1)
+
+    def ask_for(k, carry):
+        p = lax.rem(me + k, DEV)
+        pltpu.make_async_remote_copy(
+            src_ref=asked.at[p], dst_ref=asks.at[me], send_sem=sems.at[2], recv_sem=sems.at[3],
+            device_id=device(p), device_id_type=MESH,
+        ).start()
+        return carry
+
+    lax.fori_loop(1, DEV, ask_for, 0)
+    tallies = []
+    for k in range(1, NB):
+        tally = pltpu.make_async_remote_copy(
+            src_ref=count_out, dst_ref=count_in.at[b], send_sem=count_send.at[k],
+            recv_sem=count_recv.at[k], device_id=(lax.rem(b + k, NB), g), device_id_type=MESH,
+        )
+        tally.start()
+        tallies.append(tally)
+    load.wait()
+    wait_bytes(asks.at[pl.ds(0, DEV - 1)], sems.at[3])
+    got = asks[...].reshape(DEV, 128).astype(F32)
+    got_high = jnp.floor(got * (1.0 / 64.0))
+    got_low = got - 64.0 * got_high
+    spread = hot(iota((SLOTS, DEV), 0) // CAP == iota((SLOTS, DEV), 1))
+    every = 64.0 * dot(spread, got_high.astype(BF)) + dot(spread, got_low.astype(BF))
+    pick = lax.rem(iota((SLOTS, 128), 0), CAP) * 16 == iota((SLOTS, 128), 1)
+    want = jnp.sum(jnp.where(pick, every, 0.0), axis=1, keepdims=True) - 1.0
+    want = jnp.broadcast_to(want, (SLOTS, 128))
+    want_v[...] = want.astype(jnp.int32)
+    want_ref[...] = want.T[:8].astype(jnp.int32)
+    part = SLOTS // 4
+    peers = DEV // 4
+
+    def serve(i, carry):
+        c = lax.rem(me // peers + i, 4)
+        rows = want_v[pl.ds(pl.multiple_of(c * part, part), part), :]
+        chosen = hot(rows[:, :1] == iota((part, ROWS), 1))
+        found = paired_halves(dot(chosen, table_v[...]))
+        rows_out[pl.ds(pl.multiple_of(c * 2 * part, 2 * part), 2 * part), :] = found
+
+        def give(k, inner):
+            p = c * peers + lax.rem(me + k, peers)
+
+            @pl.when(p != me)
+            def _():
+                pltpu.make_async_remote_copy(
+                    src_ref=rows_out.at[pl.ds(pl.multiple_of(p * 16, 16), 16)],
+                    dst_ref=rows_in.at[pl.ds(pl.multiple_of(me * 16, 16), 16)],
+                    send_sem=sems.at[4], recv_sem=sems.at[5],
+                    device_id=device(p), device_id_type=MESH,
+                ).start()
+
+            return inner
+
+        return lax.fori_loop(0, peers, give, carry)
+
+    lax.fori_loop(0, 4, serve, 0)
+    home = pl.ds(pl.multiple_of(me * 16, 16), 16)
+    own = pltpu.make_async_copy(rows_out.at[home], rows_in.at[home], sems.at[1])
+    own.start()
+    for tally in tallies:
+        tally.wait()
+    total = jnp.sum(count_in[...], axis=0)
+    start_ref[...] = total.astype(jnp.int32)
+    place = (slot.astype(jnp.int32) // CAP) * 16 + lax.rem(slot.astype(jnp.int32), CAP)
+    spots = iota((TOK, 2 * SLOTS), 1)
+    left, right = hot(place == spots), hot(place + CAP == spots)
+    own.wait()
+    wait_bytes(rows_in.at[pl.ds(0, 16 * (DEV - 1))], sems.at[5])
+    emb_ref[:, : WIDTH // 2] = dot(left, rows_in[...]).astype(BF)
+    emb_ref[:, WIDTH // 2 :] = dot(right, rows_in[...]).astype(BF)
+    wait_bytes(asked.at[pl.ds(0, DEV - 1)], sems.at[2])
+    wait_bytes(rows_out.at[pl.ds(0, 16 * (DEV - 1))], sems.at[4])
+
+
+VMEM = pl.BlockSpec(memory_space=pltpu.VMEM)
+ANY = pl.BlockSpec(memory_space=pl.ANY)
+
+
+def fetch(owner, row, seg, table):
+    return pl.pallas_call(
+        fetch_kernel,
+        out_shape=(
+            jax.ShapeDtypeStruct((TOK, WIDTH), BF),
+            jax.ShapeDtypeStruct((8, SLOTS), jnp.int32),
+            jax.ShapeDtypeStruct((8, TOK), jnp.int32),
+            jax.ShapeDtypeStruct((8, 128), jnp.int32),
+        ),
+        in_specs=[VMEM, VMEM, VMEM, ANY],
+        out_specs=(VMEM, VMEM, VMEM, VMEM),
+        scratch_shapes=[
+            pltpu.VMEM((ROWS, WIDTH), BF),
+            pltpu.VMEM((DEV, 1, 128), jnp.int32),
+            pltpu.VMEM((DEV, 1, 128), jnp.int32),
+            pltpu.VMEM((SLOTS, 128), jnp.int32),
+            pltpu.VMEM((2 * SLOTS, WIDTH // 2), BF),
+            pltpu.VMEM((2 * SLOTS, WIDTH // 2), BF),
+            pltpu.VMEM((8, 128), F32),
+            pltpu.VMEM((NB, 8, 128), F32),
+            pltpu.SemaphoreType.DMA((6,)),
+            pltpu.SemaphoreType.DMA((NB,)),
+            pltpu.SemaphoreType.DMA((NB,)),
+        ],
+        compiler_params=pltpu.CompilerParams(
+            collective_id=0, has_side_effects=True, vmem_limit_bytes=48 << 20
+        ),
+        name="fetch_rows",
+    )(owner, row, seg, table)
+
+
+def return_kernel(slot_ref, grad_ref, landed_ref, out_v, in_v, sems):
+    b, g = lax.axis_index("bal"), lax.axis_index("grp")
+    me = b * NG + g
+    barrier = greet_all(me)
+    part = SLOTS // 4
+    peers = DEV // 4
+    pl.semaphore_wait(barrier, DEV - 1)
+
+    def serve(i, carry):
+        c = lax.rem(me // peers + i, 4)
+        chosen = hot(slot_ref[:1, :] == iota((part, TOK), 0) + c * part)
+        found = paired_halves(dot(chosen, grad_ref[...]))
+        out_v[pl.ds(pl.multiple_of(c * 2 * part, 2 * part), 2 * part), :] = found
+
+        def give(k, inner):
+            p = c * peers + lax.rem(me + k, peers)
+
+            @pl.when(p != me)
+            def _():
+                pltpu.make_async_remote_copy(
+                    src_ref=out_v.at[pl.ds(pl.multiple_of(p * 16, 16), 16)],
+                    dst_ref=in_v.at[pl.ds(pl.multiple_of(me * 16, 16), 16)],
+                    send_sem=sems.at[0], recv_sem=sems.at[1],
+                    device_id=device(p), device_id_type=MESH,
+                ).start()
+
+            return inner
+
+        return lax.fori_loop(0, peers, give, carry)
+
+    lax.fori_loop(0, 4, serve, 0)
+    home = pl.ds(pl.multiple_of(me * 16, 16), 16)
+    own = pltpu.make_async_copy(out_v.at[home], in_v.at[home], sems.at[2])
+    own.start()
+    own.wait()
+    wait_bytes(in_v.at[pl.ds(0, 16 * (DEV - 1))], sems.at[1])
+    halves = in_v[...].astype(F32).reshape(DEV, 2 * CAP, WIDTH // 2)
+    whole = jnp.concatenate([halves[:, :CAP], halves[:, CAP:]], axis=2)
+    landed_ref[...] = whole.reshape(SLOTS, WIDTH).astype(BF)
+    wait_bytes(out_v.at[pl.ds(0, 16 * (DEV - 1))], sems.at[0])
+
+
+def give_back(slot, grad):
+    return pl.pallas_call(
+        return_kernel,
+        out_shape=jax.ShapeDtypeStruct((SLOTS, WIDTH), BF),
+        in_specs=[VMEM, VMEM],
+        out_specs=VMEM,
+        scratch_shapes=[
+            pltpu.VMEM((2 * SLOTS, WIDTH // 2), BF),
+            pltpu.VMEM((2 * SLOTS, WIDTH // 2), BF),
+            pltpu.SemaphoreType.DMA((3,)),
+        ],
+        compiler_params=pltpu.CompilerParams(
+            collective_id=1, has_side_effects=True, vmem_limit_bytes=48 << 20
+        ),
+        name="return_grads",
+    )(slot, grad)
+
+
+def scatter_kernel(want_ref, landed_ref, out_ref):
+    part = out_ref.shape[0]
+    rows = iota((part, SLOTS), 0) + pl.program_id(0) * part
+    out_ref[...] = dot(hot(want_ref[:1, :] == rows), landed_ref[...])
+
+
+def scatter_add(want, landed):
+    part = 256
+    return pl.pallas_call(
+        scatter_kernel,
+        grid=(ROWS // part,),
+        out_shape=jax.ShapeDtypeStruct((ROWS, WIDTH), F32),
+        in_specs=[
+            pl.BlockSpec((8, SLOTS), lambda i: (0, 0)),
+            pl.BlockSpec((SLOTS, WIDTH), lambda i: (0, 0)),
+        ],
+        out_specs=pl.BlockSpec((part, WIDTH), lambda i: (i, 0)),
+        compiler_params=pltpu.CompilerParams(vmem_limit_bytes=32 << 20),
+        name="scatter_rows",
+    )(want, landed)
 
 
 def per_device(table, item_owner, item_row, segment, w_in, w_out, cotangent):
     n_bal = lax.axis_size("bal")
-    n_grp = lax.axis_size("grp")
-    devices = n_bal * n_grp
-    owners = item_owner[0, :, 0]
     rows_here = item_row[0]
     segments = segment[0]
     upstream = cotangent[0]
     actions = rows_here.shape[0]
-    width = table.shape[1]
     hidden = w_out.shape[0]
     group_len = actions * n_bal
     len_max = group_len // 2
-    capacity = max(4, 4 * actions // devices)
-    owner_hot = (owners[:, None] == jnp.arange(devices, dtype=jnp.int32)[None, :]).astype(jnp.int32)
-    earlier = jnp.cumsum(owner_hot, axis=0) - owner_hot
-    ranks = jnp.sum(earlier * owner_hot, axis=1)
-    slots = owners * capacity + ranks
-    requests = jnp.zeros((devices * capacity,), jnp.int32).at[slots].set(rows_here)
-    wanted = send_requests(requests.reshape(devices, capacity)).reshape(-1)
-    fetched = table[wanted].reshape(devices, capacity, width)
-    arrived = send_rows(fetched).reshape(devices * capacity, width)
-    embedded = arrived[slots]
+    embedded, want, slot, _ = fetch(item_owner[0], item_row, segment, table)
     normed = layer_norm(embedded.astype(jnp.float32)).astype(jnp.bfloat16)
     pre_act = jnp.dot(normed, w_in, preferred_element_type=jnp.float32)
     activated = jax.nn.silu(pre_act)
@@ -192,11 +466,8 @@
     d_normed = lax.dot_general(d_pre, w_in, contract_cols, preferred_element_type=jnp.float32)
     _, norm_back = jax.vjp(layer_norm, embedded.astype(jnp.float32))
     d_embedded = norm_back(d_normed)[0] + upstream.astype(jnp.float32)
-    outgoing = jnp.zeros((devices * capacity, width), jnp.float32).at[slots].set(d_embedded)
-    landed = send_grads(outgoing.reshape(devices, capacity, width)).reshape(
-        devices * capacity, width
-    )
-    table_grad = jnp.zeros((table.shape[0], width), jnp.float32).at[wanted].add(landed)
+    landed = give_back(slot, d_embedded.astype(BF))
+    table_grad = scatter_add(want, landed)
     w_in_grad, w_out_grad = lax.psum((w_in_part, w_out_part), ("bal", "grp"))
     return (layer_out[None], table_grad, w_in_grad, w_out_grad)
 

time: 651 us -> 608 us (0.934)
  Pallas kernels: 0 us -> 71.1 us
  waiting for transfers between devices: 392 us -> 352 us
  other arithmetic: 32.2 us -> 9.72 us
  blocking collectives: 37.8 us -> 18.3 us
  starting transfers between devices: 14.4 us -> 0.42 us
  matrix products: 83.1 us -> 72.7 us
  local copies, waits for them, and re-layouts: 73.9 us -> 67.1 us
    pallas_call x0 -> x3, Pallas kernels: none -> 71.1 us  [the longest x1 38.9 us: fetch(): pl.pallas_call(fetch_kernel, out_shape=(jax.ShapeDtypeStruct((TOK, WIDTH)...]
    all_to_all x2 -> x0, waiting for transfers between devices: 45.3 us -> none  [the longest x1 26.5 us: send_grads(): lax.all_to_all(buffer, ('bal', 'grp'), split_axis=0, concat_axis=0, tiled...]
    all_to_all x1 -> x0, blocking collectives: 20.9 us -> none  [send_requests(): lax.all_to_all(buffer, ('bal', 'grp'), split_axis=0, concat_axis=0, tiled...]
    all_to_all x2 -> x0, starting transfers between devices: 14 us -> none  [the longest x1 9.62 us: send_grads(): lax.all_to_all(buffer, ('bal', 'grp'), split_axis=0, concat_axis=0, tiled...]
    scatter-add x1 -> x0, other arithmetic: 9.62 us -> none  [per_device(): jnp.zeros((table.shape[0], width), jnp.float32).at[wanted].add(landed)]
    psum x1, waiting for transfers between devices: 125 us -> 132 us  [per_device(): w_in_grad, w_out_grad = lax.psum((w_in_part, w_out_part), ('bal', 'grp'))]
    unnamed x39 -> x30, local copies, waits for them, and re-layouts: 14.5 us -> 15.3 us
  transfers between devices with their start and end apart: 7 -> 5, of which waited for: 7 -> 5; matrix products, arithmetic and copies ran while one was open for 3% -> 2% of each run, Pallas kernels for 0% -> 5%
where the time goes in v1:
time: 608 us; the launch traced here: 606 us
  waiting for transfers between devices  352 us (58%)
  matrix products  72.7 us (12%)
  Pallas kernels  71.1 us (12%)
  local copies, waits for them, and re-layouts  67.1 us (11%)
  blocking collectives  18.3 us (3%)
  between operations  14 us (2%)
  other arithmetic  9.72 us (2%)
    psum x1, waiting for transfers between devices, per_device(): w_in_grad, w_out_grad = lax.psum((w_in_part, w_out_part), ('bal', 'grp'))  132 us
    reduce_scatter x1, waiting for transfers between devices, per_device(): lax.psum_scatter(value_terms, 'bal', scatter_dimension=0, tiled=True)  79 us
    reduce_scatter x1, waiting for transfers between devices, per_device(): lax.psum_scatter(key_terms, 'bal', scatter_dimension=0, tiled=True)  74 us
    all_gather x1, waiting for transfers between devices, per_device(): key_part = lax.all_gather(key_rows, 'bal', axis=0, tiled=True)  43.2 us
    pallas_call x1, Pallas kernels, fetch(): pl.pallas_call(fetch_kernel, out_shape=(jax.ShapeDtypeStruct((TOK, WIDTH)...  38.9 us
    pallas_call x1, Pallas kernels, give_back(): pl.pallas_call(return_kernel, out_shape=jax.ShapeDtypeStruct((SLOTS, WIDT...  26.8 us
    all_gather x1, waiting for transfers between devices, per_device(): value_part = lax.all_gather(value_rows, 'bal', axis=0, tiled=True)  23 us
    dynamic_update_slice x8, local copies, waits for them, and re-layouts, block_step(): lax.dynamic_update_slice_in_dim(value_terms, value_piece_grad.reshape(amo...  21.4 us
  transfers between devices with their start and end apart: 5, of which 5 were waited for; matrix products, arithmetic and copies ran while one was open for 2% of the time, Pallas kernels for 5%

profile of v1, /device:TPU:1, one launch (start us, length us, event | category | flops | bytes accessed | tf_op | source)
XLA Modules:
  0.0 606.1 jit_solution(15001948629326322168)
XLA Ops:
  10.4 38.9 %fetch_rows.1 = (bf16[256,512]{1,0:T(8,128)(2,1)S(1)}, s32[8,1024]{1,0:T(8,128)S(1)}, s32[8,256]{1,0:T(8,128)S(1)}, s32[8,128]{1,0:T(8,128)}) custom-call(s32[256,1]{1,0:T(8,128)S(1)} %copy.32.owner_ref, s32[1,256]{1,0:T(1,128)S(1)} %copy-done.2, s32[1,256]{1,0:T(1,128)} %seg_ref.1, bf16[2048,512]{1,0:T(8,128)(2,1)S(1)} %copy-done.1), custom_call_target="tpu_custom_call" | custom-call | tf_op jit(solution)/shard_map/fetch_rows/pallas_call | solution.py:246
  54.3 18.3 %all-gather = s32[1,4096]{1,0:T(1,128)S(1)} all-gather(s32[1,256]{1,0:T(1,128)S(1)} %copy-done.15), channel_id=2, replica_groups=mesh['bal'=16,'grp'=8] {'bal'}, dimensions={1}, use_global_device_ids=true | all-gather | bytes 17408 | tf_op jit(solution)/shard_map/all_gather | solution.py:375
  72.7 23.0 %all-gather.4.cloned.1.call-done = bf16[4096,256]{1,0:T(8,128)(2,1)} async-done(((bf16[256,256]{1,0:T(8,128)(2,1)}), bf16[4096,256]{1,0:T(8,128)(2,1)}) %all-gather.4.cloned.1.call-update) | async-done | bytes 2097168 | tf_op jit(solution)/shard_map/all_gather | solution.py:380
  95.7 4.1 copy.34
  99.7 43.2 %all-gather.6.cloned.1.call-done = bf16[4096,256]{1,0:T(8,128)(2,1)} async-done(((bf16[256,256]{1,0:T(8,128)(2,1)}), bf16[4096,256]{1,0:T(8,128)(2,1)}) %all-gather.6.cloned.1.call-update) | async-done | bytes 2097168 | tf_op jit(solution)/shard_map/all_gather | solution.py:379
  142.9 4.1 copy.35
  147.0 17.7 %while.32 = (s32[]{:T(128)}, f32[256,4,64]{0,2,1:T(8,128)S(1)}, bf16[4096,256]{0,1:T(8,128)(2,1)}, s32[1,256]{1,0:T(1,128)S(1)}, s32[4096]{0:T(1024)S(1)}, /*ind...) while((s32[]{:T(128)}, f32[256,4,64]{0,2,1:T(8,128)S(1)}, ...), condition=%wide.region_3.4_spmd.clone, body=%wide.region_2.3_spmd.clone.sunk | while | flops 276694272 | bytes 4349125 | solution.py:53
  148.8 2.7 fusion.101
  153.2 2.7 fusion.101
  157.6 2.7 fusion.101
  162.0 2.7 fusion.101
  173.4 93.7 %while.33 = (s32[]{:T(128)}, f32[256,4,64]{0,2,1:T(8,128)}, f32[4096,256]{1,0:T(8,128)}, f32[4096,256]{1,0:T(8,128)}, bf16[4096,256]{0,1:T(8,128)(2,1)}, /*index...) while((s32[]{:T(128)}, f32[256,4,64]{0,2,1:T(8,128)}, ...), condition=%wide.region_9.10_spmd.clone, body=%wide.region_8.9_spmd.clone.sunk | while | flops 690881792 | bytes 55336276 | solution.py:53
  182.6 4.6 fusion.115
  187.2 2.5 copy.64
  189.8 2.7 fusion.116
  194.0 2.8 constant_dynamic-update-slice_fusion.3
  206.0 4.6 fusion.115
  213.2 2.7 fusion.116
  217.4 2.8 constant_dynamic-update-slice_fusion.3
  229.5 4.6 fusion.115
  236.6 2.7 fusion.116
  240.8 2.8 constant_dynamic-update-slice_fusion.3
  252.9 4.6 fusion.115
  257.5 2.5 copy.64
  260.1 2.7 fusion.116
  264.3 2.8 constant_dynamic-update-slice_fusion.3
  269.9 74.0 %reduce-scatter.5.cloned.1.call-done = f32[256,256]{1,0:T(8,128)} async-done(((f32[4096,256]{1,0:T(8,128)}), f32[256,256]{1,0:T(8,128)}) %reduce-scatter.5.cloned.1.call-update) | async-done | bytes 262160 | tf_op jit(solution)/shard_map/reduce_scatter | solution.py:452
  345.5 79.0 %reduce-scatter.3.cloned.1.call-done = f32[256,256]{1,0:T(8,128)} async-done(((f32[4096,256]{1,0:T(8,128)}), f32[256,256]{1,0:T(8,128)}) %reduce-scatter.3.cloned.1.call-update) | async-done | bytes 262160 | tf_op jit(solution)/shard_map/reduce_scatter | solution.py:453
  431.8 26.8 %return_grads.1.landed_ref = bf16[1024,512]{1,0:T(8,128)(2,1)S(1)} custom-call(s32[8,256]{1,0:T(8,128)S(1)} %get-tuple-element.335.slot_ref, bf16[256,512]{1,0:T(8,128)(2,1)S(1)} %add_convert_fusion.grad_ref), custom_call_target="tpu_custom_call" | custom-call | tf_op jit(solution)/shard_map/return_grads/pallas_call | solution.py:319
  458.6 5.4 scatter_rows.1
  463.9 131.6 %all-reduce.3.cloned.1.call-done = (f32[512,1024]{1,0:T(8,128)}, f32[256,512]{1,0:T(8,128)}) async-done(((f32[512,1024]{1,0:T(8,128)}, f32[256,512]{1,0:T(8,128)}), (f32[512,1024]{1,0:T(8,128)}, f32[256,512]{1,0:T(8,128)})) %all-reduce.3.cloned.1.call-update) | async-done | bytes 2621456 | tf_op jit(solution)/shard_map/psum | solution.py:471
  595.5 3.2 copy.89
  (166 shorter events, 83.6 us)
Async XLA Ops:
  7.2 42.5 %copy-start = (bf16[512,1024]{1,0:T(8,128)(2,1)S(1)}, bf16[512,1024]{1,0:T(8,128)(2,1)}, u32[]{:S(2)}) copy-start(bf16[512,1024]{1,0:T(8,128)(2,1)} %param.15) | copy-start | bytes 3145732
  7.2 88.5 %all-gather.4.cloned.1.call-start = ((), (), s32[]{:S(2)}) async-start(), calls=%async_computation.2 | async-start | bytes 2228224 | tf_op jit(solution)/shard_map/all_gather | solution.py:380
  8.1 1.6 copy-start.1
  49.3 5.0 copy-start.15
  52.7 90.2 %all-gather.6.cloned.1.call-start = ((), (), s32[]{:S(2)}) async-start(), calls=%async_computation.3 | async-start | bytes 2228224 | tf_op jit(solution)/shard_map/all_gather | solution.py:379
  53.5 290.4 %reduce-scatter.5.cloned.1.call-start = ((), (), s32[]{:S(2)}) async-start(), calls=%async_computation.5 | async-start | bytes 4456448 | tf_op jit(solution)/shard_map/reduce_scatter | solution.py:452
  147.0 17.9 %copy-start.7 = (bf16[1,256,512]{2,1,0:T(8,128)(2,1)S(1)}, bf16[1,256,512]{2,1,0:T(8,128)(2,1)}, u32[]{:S(2)}) copy-start(bf16[1,256,512]{2,1,0:T(8,128)(2,1)} %param.17) | copy-start | bytes 786436
  147.0 17.9 %copy-start.11 = (bf16[256,512]{1,0:T(8,128)(2,1)S(1)}, bf16[256,512]{1,0:T(8,128)(2,1)}, u32[]{:S(2)}) copy-start(bf16[256,512]{1,0:T(8,128)(2,1)} %param.16) | copy-start | bytes 786436
  173.4 4.8 copy-start.16
  174.5 3.4 copy-start.3
  176.4 4.0 copy-start.4
  178.3 2.1 copy-start.6
  196.8 4.8 copy-start.16
  197.9 3.4 copy-start.3
  199.7 4.0 copy-start.4
  201.6 2.1 copy-start.6
  220.2 4.8 copy-start.16
  221.3 3.4 copy-start.3
  223.2 4.0 copy-start.4
  225.1 2.1 copy-start.6
  243.7 4.8 copy-start.16
  244.8 3.4 copy-start.3
  246.6 4.0 copy-start.4
  248.5 2.1 copy-start.6
  267.1 0.9 copy-start.5
  267.1 1.7 copy-start.8
  267.1 1.7 copy-start.9
  267.1 158.3 %copy-start.10 = (f32[256,1024]{1,0:T(8,128)S(1)}, f32[256,1024]{1,0:T(8,128)}, u32[]{:S(2)}) copy-start(f32[256,1024]{1,0:T(8,128)} %get-tuple-element.500) | copy-start | bytes 3145732
  267.1 158.3 %copy-start.13 = (bf16[256,256]{1,0:T(8,128)(2,1)S(1)}, bf16[256,256]{1,0:T(8,128)(2,1)}, u32[]{:S(2)}) copy-start(bf16[256,256]{1,0:T(8,128)(2,1)} %get-tuple-element.493) | copy-start | bytes 393220
  267.1 157.3 %reduce-scatter.3.cloned.1.call-start = ((), (), s32[]{:S(2)}) async-start(), calls=%async_computation.4 | async-start | bytes 4456448 | tf_op jit(solution)/shard_map/reduce_scatter | solution.py:453
  267.7 327.8 %all-reduce.3.cloned.1.call-start = ((), (), s32[]{:S(2)}) async-start(), calls=%async_computation.6 | async-start | bytes 5242880 | tf_op jit(solution)/shard_map/psum | solution.py:471
  595.5 3.2 copy-start.14
  (2 other events, 1.5 us)
Sparse Core Ops, SparseCore 0:
  52.9 42.7 all-gather.3
  98.4 44.5 all-gather.5
  267.2 76.5 reduce-scatter.4
  347.4 76.9 reduce-scatter.2
  429.9 165.6 all-reduce.2

commit v2 on v1

--- a/solution.py
+++ b/solution.py
@@ -4,59 +4,6 @@
 from jax.experimental import pallas as pl
 from jax.experimental.pallas import tpu as pltpu
 from jax.sharding import PartitionSpec as P
-
-HEADS = 4
-DH = 64
-
-
-norm_eps = 1e-06
-contract_rows = (((0,), (0,)), ((), ()))
-contract_cols = (((1,), (1,)), ((), ()))
-
-
-def layer_norm(values):
-    average = jnp.mean(values, axis=-1, keepdims=True)
-    centred = values - average
-    spread = jnp.mean(centred * centred, axis=-1, keepdims=True)
-    return centred * lax.rsqrt(spread + norm_eps)
-
-
-def output_norm(attended, gate):
-    return layer_norm(attended) * gate
-
-
-def silu_slope(values):
-    sigmoids = jax.nn.sigmoid(values)
-    return sigmoids * (1.0 + values * (1.0 - sigmoids))
-
-
-def by_heads(values):
-    return values.reshape(values.shape[0], HEADS, DH)
-
-
-def visible_pairs(query_pos, query_seg, key_pos, key_seg):
-    return (query_seg[:, None] == key_seg[None, :]) & (key_pos[None, :] <= query_pos[:, None])
-
-
-def pair_terms(queries, keys_in, visible, len_max):
-    scores = jnp.einsum("qhd,khd->hqk", queries, keys_in, preferred_element_type=jnp.float32)
-    sigmoids = jax.nn.sigmoid(scores)
-    weight = jnp.where(visible[None], scores * sigmoids / len_max, 0.0)
-    slopes = jnp.where(visible[None], sigmoids * (1.0 + scores * (1.0 - sigmoids)) / len_max, 0.0)
-    return (weight, slopes)
-
-
-def sweep(block_step, carry, amount):
-    block = amount
-    while block > 1024 and block % 2 == 0:
-        block = block // 2
-    return lax.fori_loop(
-        0,
-        amount // block,
-        lambda counter, current: block_step(current, counter * block, block),
-        carry,
-    )
-
 
 MESH = pl.DeviceIdType.MESH
 BF = jnp.bfloat16
@@ -273,6 +220,350 @@
     )(owner, row, seg, table)
 
 
+HEADS = 4
+DH = 64
+HD = HEADS * DH
+GROUP = TOK * NB
+NORM_EPS = 1e-06
+SPAN = 3
+
+
+def dot_rows(a, b):
+    return lax.dot_general(a, b, (((0,), (0,)), ((), ())), preferred_element_type=F32)
+
+
+def fold(rows):
+    half = rows.shape[0] // 2
+    return jnp.concatenate([rows[:half], rows[half:]], axis=1)
+
+
+def unfold(rows):
+    return jnp.concatenate([rows[:, :DH], rows[:, DH:]], axis=0)
+
+
+def normalise(values):
+    centred = values - jnp.mean(values, axis=-1, keepdims=True)
+    scale = lax.rsqrt(jnp.mean(centred * centred, axis=-1, keepdims=True) + NORM_EPS)
+    return centred * scale, scale
+
+
+def norm_grad(grad, normed, scale):
+    along = jnp.mean(grad * normed, axis=-1, keepdims=True)
+    return scale * (grad - jnp.mean(grad, axis=-1, keepdims=True) - normed * along)
+
+
+def tile(i, size=TOK):
+    return pl.ds(pl.multiple_of(i * size, size), size)
+
+
+def layer_kernel(
+    emb_ref, start_ref, w_in_ref, w_out_ref, cot_ref,
+    out_ref, demb_ref, w_in_part, w_out_part,
+    slope_v, gate_v, kv_out, q_out, kv_in, q_in, q_v, qt_v, begin_v,
+    w_v, s_v, att_v, att_out, att_in, d_out, d_in, dt_v, dq_v, dq_out, dq_in,
+    g_out, g_in, joined,
+    kv_send, kv_recv, q_send, q_recv, a_send, a_recv, d_send, d_recv,
+    g_send, g_recv, e_send, e_recv,
+):
+    b, g = lax.axis_index("bal"), lax.axis_index("grp")
+    z, x = b // HEADS, lax.rem(b, HEADS)
+    barrier = pltpu.get_barrier_semaphore()
+    for k in range(1, NB):
+        pl.semaphore_signal(
+            barrier, inc=1, device_id=(lax.rem(b + k, NB), g), device_id_type=MESH
+        )
+
+    def remote(src, dst, send, recv, at_z, at_x):
+        return pltpu.make_async_remote_copy(
+            src_ref=src, dst_ref=dst, send_sem=send, recv_sem=recv,
+            device_id=(at_z * HEADS + at_x, g), device_id_type=MESH,
+        )
+
+    def spread(out, into, send, recv):
+        for h in range(HEADS):
+            @pl.when(h != x)
+            def _():
+                remote(out.at[h], into.at[x], send.at[h], recv.at[x], z, h).start()
+
+            @pl.when(h == x)
+            def _():
+                into[h] = out[h]
+
+    def collect(out, into, send, recv):
+        for h in range(HEADS):
+            @pl.when(h != x)
+            def _():
+                remote(out.at[h], into.at[h], send.at[h], recv.at[h], z, h).wait_recv()
+
+    def sent(out, into, send, recv):
+        for h in range(HEADS):
+            @pl.when(h != x)
+            def _():
+                remote(out.at[h], into.at[h], send.at[h], recv.at[h], z, h).wait_send()
+
+    embedded = emb_ref[...].astype(F32)
+    normed, _ = normalise(embedded)
+    normed = normed.astype(BF)
+    pre = dot(normed, w_in_ref[...])
+    sig = jax.nn.sigmoid(pre)
+    act = pre * sig
+    gate_v[...] = act[:, :HD].astype(BF)
+    for h in range(HEADS):
+        value, query, key = (
+            act[:, part * HD + h * DH : part * HD + (h + 1) * DH] for part in (1, 2, 3)
+        )
+        kv_out[h] = jnp.concatenate([key, value], axis=1).astype(BF)
+        q_out[h] = fold(query * 0.5).astype(BF)
+    pl.semaphore_wait(barrier, NB - 1)
+    spread(q_out, q_in, q_send, q_recv)
+    for dz in range(SPAN):
+        for h in range(HEADS):
+            @pl.when((z + dz < HEADS) & ((h != x) | (dz > 0)))
+            def _():
+                remote(
+                    kv_out.at[h], kv_in.at[dz, x], kv_send.at[dz, h], kv_recv.at[dz, x], z + dz, h
+                ).start()
+
+            if dz == 0:
+                @pl.when(h == x)
+                def _():
+                    kv_in[0, h] = kv_out[h]
+
+    slope_v[...] = sig * (1.0 + pre * (1.0 - sig))
+    att_v[...] = jnp.zeros_like(att_v)
+    dq_v[...] = jnp.zeros_like(dq_v)
+    places = z * HEADS * TOK + iota((HEADS * TOK, 128), 0)
+    starts = start_ref[:1, :]
+    begin = jnp.max(jnp.where(starts <= places, starts, 0).astype(F32), axis=1, keepdims=True)
+    begin_v[...] = jnp.broadcast_to(begin, (HEADS * TOK, 128)).astype(jnp.int32)
+    collect(q_out, q_in, q_send, q_recv)
+    for h in range(HEADS):
+        q = unfold(q_in[h].astype(F32))
+        q_v[h * TOK : (h + 1) * TOK, :] = jnp.concatenate(
+            [q, jnp.zeros((TOK, DH), F32)], axis=1
+        ).astype(BF)
+        qt_v[:, h * TOK : (h + 1) * TOK] = q.T.astype(BF)
+
+    def forward_pair(dz, i, j):
+        kv = kv_in[dz, j]
+        scores = dot_t(q_v[tile(i), :], kv)
+        half = jnp.tanh(scores)
+        more = 1.0 + half
+        key_pos = ((z - dz) * HEADS + j) * TOK + iota((TOK, TOK), 1)
+        visible = key_pos >= begin_v[tile(i), :1]
+        if dz == 0:
+            visible &= key_pos <= (z * HEADS + i) * TOK + iota((TOK, TOK), 0)
+        weight = jnp.where(visible, scores * more, 0.0).astype(BF)
+        w_v[dz, i * HEADS + j] = weight
+        s_v[dz, i * HEADS + j] = jnp.where(
+            visible, more * (1.0 + scores * (1.0 - half)), 0.0
+        ).astype(BF)
+        att_v[tile(i), :] += dot(weight, kv)
+
+    def arrived(dz):
+        for h in range(HEADS):
+            def arrival():
+                remote(
+                    kv_out.at[h], kv_in.at[dz, h], kv_send.at[dz, h], kv_recv.at[dz, h], z, h
+                ).wait_recv()
+
+            if dz == 0:
+                pl.when(h != x)(arrival)
+            else:
+                arrival()
+
+    def sweep(body, dz):
+        def outer(i, carry):
+            low = 0 if dz < 2 else i
+            high = i + 1 if dz == 0 else HEADS
+
+            def inner(j, carry):
+                body(dz, i, j)
+                return carry
+
+            return lax.fori_loop(low, high, inner, carry)
+
+        lax.fori_loop(0, HEADS, outer, 0)
+
+    for dz in range(SPAN):
+        @pl.when(z >= dz)
+        def _():
+            arrived(dz)
+            sweep(forward_pair, dz)
+
+    for h in range(HEADS):
+        att = att_v[h * TOK : (h + 1) * TOK, DH:] * (2.0 / GROUP)
+        att_out[h] = fold(att).astype(BF)
+    spread(att_out, att_in, a_send, a_recv)
+    cot = cot_ref[...]
+    d_mixed = dot_t(cot, w_out_ref[...])
+    gate = gate_v[...].astype(F32)
+    collect(att_out, att_in, a_send, a_recv)
+
+    attended = jnp.concatenate([unfold(att_in[h].astype(F32)) for h in range(HEADS)], axis=1)
+    level, scale = normalise(attended)
+    delta = norm_grad(d_mixed * gate, level, scale)
+    for h in range(HEADS):
+        d_out[h] = fold(delta[:, h * DH : (h + 1) * DH]).astype(BF)
+    spread(d_out, d_in, d_send, d_recv)
+    mixed = (level * gate).astype(BF)
+    out_ref[...] = (dot(mixed, w_out_ref[...]) + emb_ref[...].astype(F32)).astype(BF)
+    w_out_part[...] = dot_rows(mixed, cot).astype(w_out_part.dtype)
+    joined[:, :HD] = (d_mixed * level).astype(BF)
+    collect(d_out, d_in, d_send, d_recv)
+    for h in range(HEADS):
+        d = unfold(d_in[h].astype(F32))
+        q_v[HEADS * TOK + h * TOK : HEADS * TOK + (h + 1) * TOK, :] = jnp.concatenate(
+            [jnp.zeros((TOK, DH), F32), d], axis=1
+        ).astype(BF)
+        dt_v[:, h * TOK : (h + 1) * TOK] = d.T.astype(BF)
+
+    def backward(dz):
+        def keys(j, carry):
+            kv = kv_in[dz, j]
+
+            def queries(i, grads):
+                dk, dv = grads
+                product = dot_t(q_v[tile(HEADS + i), :], kv)
+                d_score = (product * s_v[dz, i * HEADS + j].astype(F32)).astype(BF)
+                dq_v[tile(i), :] += dot(d_score, kv)
+                dk = dk + dot(qt_v[:, tile(i)], d_score)
+                dv = dv + dot(dt_v[:, tile(i)], w_v[dz, i * HEADS + j])
+                return dk, dv
+
+            low = j if dz == 0 else 0
+            high = j + 1 if dz == 2 else HEADS
+            zeros = jnp.zeros((DH, TOK), F32)
+            dk, dv = lax.fori_loop(low, high, queries, (zeros, zeros))
+            grads = jnp.concatenate([dk, dv], axis=0) * (2.0 / GROUP)
+            g_out[dz, j] = grads.T.astype(BF)
+            if dz == 0:
+                @pl.when(j != x)
+                def _():
+                    remote(
+                        g_out.at[0, j], g_in.at[0, x], g_send.at[0, j], g_recv.at[0, x], z, j
+                    ).start()
+
+                @pl.when(j == x)
+                def _():
+                    g_in[0, j] = g_out[0, j]
+            else:
+                remote(
+                    g_out.at[dz, j], g_in.at[dz, x], g_send.at[dz, j], g_recv.at[dz, x], z - dz, j
+                ).start()
+            return carry
+
+        lax.fori_loop(0, HEADS, keys, 0)
+
+    for dz in reversed(range(SPAN)):
+        @pl.when(z >= dz)
+        def _():
+            backward(dz)
+
+    for h in range(HEADS):
+        dq_out[h] = fold(dq_v[h * TOK : (h + 1) * TOK, :DH] * (1.0 / GROUP)).astype(BF)
+    spread(dq_out, dq_in, e_send, e_recv)
+
+    embedded = emb_ref[...].astype(F32)
+    spread_in, spread_scale = normalise(embedded)
+    normed = spread_in.astype(BF)
+    for dz in reversed(range(SPAN)):
+        for h in range(HEADS):
+            def arrival():
+                remote(
+                    g_out.at[dz, h], g_in.at[dz, h], g_send.at[dz, h], g_recv.at[dz, h], z, h
+                ).wait_recv()
+
+            if dz == 0:
+                pl.when(h != x)(arrival)
+            else:
+                pl.when(z + dz < HEADS)(arrival)
+
+    collect(dq_out, dq_in, e_send, e_recv)
+    for h in range(HEADS):
+        total = g_in[0, h].astype(F32)
+        for dz in range(1, SPAN):
+            total += jnp.where(z + dz < HEADS, g_in[dz, h].astype(F32), 0.0)
+        joined[:, HD + h * DH : HD + (h + 1) * DH] = total[:, DH:].astype(BF)
+        joined[:, 2 * HD + h * DH : 2 * HD + (h + 1) * DH] = unfold(
+            dq_in[h].astype(F32)
+        ).astype(BF)
+        joined[:, 3 * HD + h * DH : 3 * HD + (h + 1) * DH] = total[:, :DH].astype(BF)
+    d_pre = (joined[...].astype(F32) * slope_v[...]).astype(BF)
+    w_in_part[...] = dot_rows(normed, d_pre).astype(w_in_part.dtype)
+    d_normed = dot_t(d_pre, w_in_ref[...])
+    demb_ref[...] = (
+        norm_grad(d_normed, spread_in, spread_scale) + cot_ref[...].astype(F32)
+    ).astype(BF)
+
+    sent(q_out, q_in, q_send, q_recv)
+    sent(att_out, att_in, a_send, a_recv)
+    sent(d_out, d_in, d_send, d_recv)
+    sent(dq_out, dq_in, e_send, e_recv)
+    for dz in range(SPAN):
+        for h in range(HEADS):
+            @pl.when((z + dz < HEADS) & ((h != x) | (dz > 0)))
+            def _():
+                remote(
+                    kv_out.at[h], kv_in.at[dz, h], kv_send.at[dz, h], kv_recv.at[dz, h], z, h
+                ).wait_send()
+
+            @pl.when((z >= dz) & ((h != x) | (dz > 0)))
+            def _():
+                remote(
+                    g_out.at[dz, h], g_in.at[dz, h], g_send.at[dz, h], g_recv.at[dz, h], z, h
+                ).wait_send()
+
+
+def layer(embedded, start, w_in, w_out, cot, part_type):
+    dma = pltpu.SemaphoreType.DMA
+    return pl.pallas_call(
+        layer_kernel,
+        out_shape=(
+            jax.ShapeDtypeStruct((TOK, WIDTH), BF),
+            jax.ShapeDtypeStruct((TOK, WIDTH), BF),
+            jax.ShapeDtypeStruct((WIDTH, 4 * HD), part_type),
+            jax.ShapeDtypeStruct((HD, WIDTH), part_type),
+        ),
+        in_specs=[VMEM] * 5,
+        out_specs=(VMEM,) * 4,
+        scratch_shapes=[
+            pltpu.VMEM((TOK, 4 * HD), F32),
+            pltpu.VMEM((TOK, HD), BF),
+            pltpu.VMEM((HEADS, TOK, 2 * DH), BF),
+            pltpu.VMEM((HEADS, TOK // 2, 2 * DH), BF),
+            pltpu.VMEM((SPAN, HEADS, TOK, 2 * DH), BF),
+            pltpu.VMEM((HEADS, TOK // 2, 2 * DH), BF),
+            pltpu.VMEM((2 * HEADS * TOK, 2 * DH), BF),
+            pltpu.VMEM((DH, HEADS * TOK), BF),
+            pltpu.VMEM((HEADS * TOK, 128), jnp.int32),
+            pltpu.VMEM((SPAN, HEADS * HEADS, TOK, TOK), BF),
+            pltpu.VMEM((SPAN, HEADS * HEADS, TOK, TOK), BF),
+            pltpu.VMEM((HEADS * TOK, 2 * DH), F32),
+            pltpu.VMEM((HEADS, TOK // 2, 2 * DH), BF),
+            pltpu.VMEM((HEADS, TOK // 2, 2 * DH), BF),
+            pltpu.VMEM((HEADS, TOK // 2, 2 * DH), BF),
+            pltpu.VMEM((HEADS, TOK // 2, 2 * DH), BF),
+            pltpu.VMEM((DH, HEADS * TOK), BF),
+            pltpu.VMEM((HEADS * TOK, 2 * DH), F32),
+            pltpu.VMEM((HEADS, TOK // 2, 2 * DH), BF),
+            pltpu.VMEM((HEADS, TOK // 2, 2 * DH), BF),
+            pltpu.VMEM((SPAN, HEADS, TOK, 2 * DH), BF),
+            pltpu.VMEM((SPAN, HEADS, TOK, 2 * DH), BF),
+            pltpu.VMEM((TOK, 4 * HD), BF),
+            dma((SPAN, HEADS)),
+            dma((SPAN, HEADS)),
+        ]
+        + [dma((HEADS,))] * 6
+        + [dma((SPAN, HEADS))] * 2
+        + [dma((HEADS,))] * 2,
+        compiler_params=pltpu.CompilerParams(
+            collective_id=2, has_side_effects=True, vmem_limit_bytes=56 << 20
+        ),
+        name="layer",
+    )(embedded, start, w_in, w_out, cot)
+
+
 def return_kernel(slot_ref, grad_ref, landed_ref, out_v, in_v, sems):
     b, g = lax.axis_index("bal"), lax.axis_index("grp")
     me = b * NG + g
@@ -356,117 +647,11 @@
 
 
 def per_device(table, item_owner, item_row, segment, w_in, w_out, cotangent):
-    n_bal = lax.axis_size("bal")
-    rows_here = item_row[0]
-    segments = segment[0]
-    upstream = cotangent[0]
-    actions = rows_here.shape[0]
-    hidden = w_out.shape[0]
-    group_len = actions * n_bal
-    len_max = group_len // 2
-    embedded, want, slot, _ = fetch(item_owner[0], item_row, segment, table)
-    normed = layer_norm(embedded.astype(jnp.float32)).astype(jnp.bfloat16)
-    pre_act = jnp.dot(normed, w_in, preferred_element_type=jnp.float32)
-    activated = jax.nn.silu(pre_act)
-    gate = activated[:, :hidden].astype(jnp.bfloat16)
-    value_rows = activated[:, hidden : 2 * hidden].astype(jnp.bfloat16)
-    query_rows = activated[:, 2 * hidden : 3 * hidden].astype(jnp.bfloat16)
-    key_rows = activated[:, 3 * hidden :].astype(jnp.bfloat16)
-    all_segments = lax.all_gather(segments, "bal", axis=0, tiled=True)
-    my_pos = lax.axis_index("bal") * actions + jnp.arange(actions, dtype=jnp.int32)
-    query_heads = by_heads(query_rows)
-    head_zeros = jnp.zeros((actions, HEADS, DH), jnp.float32)
-    key_part = lax.all_gather(key_rows, "bal", axis=0, tiled=True)
-    value_part = lax.all_gather(value_rows, "bal", axis=0, tiled=True)
-
-    def block_step(running, offset, amount):
-        key_block = by_heads(lax.dynamic_slice_in_dim(key_part, offset, amount, 0))
-        value_block = by_heads(lax.dynamic_slice_in_dim(value_part, offset, amount, 0))
-        key_pos = offset + jnp.arange(amount, dtype=jnp.int32)
-        key_seg = lax.dynamic_slice_in_dim(all_segments, offset, amount, 0)
-        weight, _ = pair_terms(
-            query_heads, key_block, visible_pairs(my_pos, segments, key_pos, key_seg), len_max
-        )
-        return running + jnp.einsum(
-            "hqk,khd->qhd",
-            weight.astype(jnp.bfloat16),
-            value_block,
-            preferred_element_type=jnp.float32,
-        )
-
-    attended = sweep(block_step, head_zeros, key_part.shape[0]).reshape(actions, hidden)
-    mixed, post_back = jax.vjp(output_norm, attended, gate.astype(jnp.float32))
-    mixed_low = mixed.astype(jnp.bfloat16)
-    layer_out = (
-        jnp.dot(mixed_low, w_out, preferred_element_type=jnp.float32) + embedded.astype(jnp.float32)
-    ).astype(jnp.bfloat16)
-    w_out_part = lax.dot_general(
-        mixed_low, upstream, contract_rows, preferred_element_type=jnp.float32
+    embedded, want, slot, start = fetch(item_owner[0], item_row, segment, table)
+    layer_out, d_embedded, w_in_part, w_out_part = layer(
+        embedded, start, w_in, w_out, cotangent[0], F32
     )
-    d_mixed = lax.dot_general(upstream, w_out, contract_cols, preferred_element_type=jnp.float32)
-    d_attended, d_gate = post_back(d_mixed)
-    deltas = d_attended.astype(jnp.bfloat16)
-    gate_grad = d_gate.astype(jnp.bfloat16)
-    delta_heads = by_heads(deltas)
-    group_zeros = jnp.zeros((group_len, hidden), jnp.float32)
-    joint_key_part = lax.all_gather(key_rows, "bal", axis=0, tiled=True)
-    joint_value_part = lax.all_gather(value_rows, "bal", axis=0, tiled=True)
-
-    def block_step(running, offset, amount):
-        query_total, key_terms, value_terms = running
-        key_block = by_heads(lax.dynamic_slice_in_dim(joint_key_part, offset, amount, 0))
-        value_block = by_heads(lax.dynamic_slice_in_dim(joint_value_part, offset, amount, 0))
-        key_pos = offset + jnp.arange(amount, dtype=jnp.int32)
-        key_seg = lax.dynamic_slice_in_dim(all_segments, offset, amount, 0)
-        weight, slopes = pair_terms(
-            query_heads, key_block, visible_pairs(my_pos, segments, key_pos, key_seg), len_max
-        )
-        product = jnp.einsum(
-            "qhd,khd->hqk", delta_heads, value_block, preferred_element_type=jnp.float32
-        )
-        d_score = (product * slopes).astype(jnp.bfloat16)
-        query_total = query_total + jnp.einsum(
-            "hqk,khd->qhd", d_score, key_block, preferred_element_type=jnp.float32
-        )
-        key_piece_grad = jnp.einsum(
-            "hqk,qhd->khd", d_score, query_heads, preferred_element_type=jnp.float32
-        )
-        value_piece_grad = jnp.einsum(
-            "hqk,qhd->khd",
-            weight.astype(jnp.bfloat16),
-            delta_heads,
-            preferred_element_type=jnp.float32,
-        )
-        key_terms = lax.dynamic_update_slice_in_dim(
-            key_terms, key_piece_grad.reshape(amount, hidden), offset, 0
-        )
-        value_terms = lax.dynamic_update_slice_in_dim(
-            value_terms, value_piece_grad.reshape(amount, hidden), offset, 0
-        )
-        return (query_total, key_terms, value_terms)
-
-    query_grad, key_terms, value_terms = sweep(
-        block_step, (head_zeros, group_zeros, group_zeros), joint_key_part.shape[0]
-    )
-    key_grad, value_grad = (
-        lax.psum_scatter(key_terms, "bal", scatter_dimension=0, tiled=True),
-        lax.psum_scatter(value_terms, "bal", scatter_dimension=0, tiled=True),
-    )
-    joined = jnp.concatenate(
-        [
-            gate_grad,
-            value_grad.astype(jnp.bfloat16),
-            query_grad.reshape(actions, hidden).astype(jnp.bfloat16),
-            key_grad.astype(jnp.bfloat16),
-        ],
-        axis=1,
-    )
-    d_pre = (joined.astype(jnp.float32) * silu_slope(pre_act)).astype(jnp.bfloat16)
-    w_in_part = lax.dot_general(normed, d_pre, contract_rows, preferred_element_type=jnp.float32)
-    d_normed = lax.dot_general(d_pre, w_in, contract_cols, preferred_element_type=jnp.float32)
-    _, norm_back = jax.vjp(layer_norm, embedded.astype(jnp.float32))
-    d_embedded = norm_back(d_normed)[0] + upstream.astype(jnp.float32)
-    landed = give_back(slot, d_embedded.astype(BF))
+    landed = give_back(slot, d_embedded)
     table_grad = scatter_add(want, landed)
     w_in_grad, w_out_grad = lax.psum((w_in_part, w_out_part), ("bal", "grp"))
     return (layer_out[None], table_grad, w_in_grad, w_out_grad)

time: 608 us -> 282 us (0.46)
  waiting for transfers between devices: 352 us -> 132 us
  matrix products: 72.7 us -> 0 us
  local copies, waits for them, and re-layouts: 67.1 us -> 10.7 us
  Pallas kernels: 71.1 us -> 125 us
  blocking collectives: 18.3 us -> 0 us
  other arithmetic: 9.72 us -> 0 us
    reduce_scatter x2 -> x0, waiting for transfers between devices: 153 us -> none  [the longest x1 79 us: per_device(): lax.psum_scatter(value_terms, 'bal', scatter_dimension=0, tiled=True)]
    dot_general x30 -> x0, matrix products: 72.7 us -> none  [the longest x4 18.5 us: block_step(): jnp.einsum('hqk,qhd->khd', weight.astype(jnp.bfloat16), delta_heads, pref...]
    all_gather x2 -> x0, waiting for transfers between devices: 66.2 us -> none  [the longest x1 43.2 us: per_device(): key_part = lax.all_gather(key_rows, 'bal', axis=0, tiled=True)]
    pallas_call x0 -> x1, Pallas kernels: none -> 40.9 us  [layer(): pl.pallas_call(layer_kernel, out_shape=(jax.ShapeDtypeStruct((TOK, WIDTH)...]
    dynamic_update_slice x12 -> x0, local copies, waits for them, and re-layouts: 27.6 us -> none  [the longest x8 21.4 us: block_step(): lax.dynamic_update_slice_in_dim(value_terms, value_piece_grad.reshape(amo...]
    all_gather x1 -> x0, blocking collectives: 18.3 us -> none  [per_device(): all_segments = lax.all_gather(segments, 'bal', axis=0, tiled=True)]
    dynamic_slice x20 -> x0, local copies, waits for them, and re-layouts: 15.6 us -> none  [the longest x4 5.94 us: block_step(): lax.dynamic_slice_in_dim(joint_value_part, offset, amount, 0)]
    pallas_call x1, Pallas kernels: 26.8 us -> 41 us  [give_back(): pl.pallas_call(return_kernel, out_shape=jax.ShapeDtypeStruct((SLOTS, WIDT...]
  transfers between devices with their start and end apart: 5 -> 1, of which waited for: 5 -> 1; matrix products, arithmetic and copies ran while one was open for 2% -> 0% of each run, Pallas kernels for 5% -> 16%
where the time goes in v2:
time: 282 us; the launch traced here: 281 us
  waiting for transfers between devices  132 us (47%)
  Pallas kernels  125 us (44%)
  between operations  14.1 us (5%)
  local copies, waits for them, and re-layouts  10.7 us (4%)
    psum x1, waiting for transfers between devices, per_device(): w_in_grad, w_out_grad = lax.psum((w_in_part, w_out_part), ('bal', 'grp'))  132 us
    pallas_call x1, Pallas kernels, give_back(): pl.pallas_call(return_kernel, out_shape=jax.ShapeDtypeStruct((SLOTS, WIDT...  41 us
    pallas_call x1, Pallas kernels, layer(): pl.pallas_call(layer_kernel, out_shape=(jax.ShapeDtypeStruct((TOK, WIDTH)...  40.9 us
    pallas_call x1, Pallas kernels, fetch(): pl.pallas_call(fetch_kernel, out_shape=(jax.ShapeDtypeStruct((TOK, WIDTH)...  37.7 us
    unnamed x19, local copies, waits for them, and re-layouts  9.87 us
  transfers between devices with their start and end apart: 1, of which 1 were waited for; matrix products, arithmetic and copies ran while one was open for 0% of the time, Pallas kernels for 16%

profile of v2, /device:TPU:1, one launch (start us, length us, event | category | flops | bytes accessed | tf_op | source)
XLA Modules:
  0.0 281.4 jit_solution(10344433349881285343)
XLA Ops:
  7.2 0.0 all-reduce.3.cloned.1.call-start
  7.2 0.8 copy.11.owner_ref
  8.0 0.0 copy-start
  8.0 1.6 copy-done
  9.6 0.0 copy-start.4
  9.6 0.7 copy-done.4
  10.3 0.0 copy-start.5
  10.3 0.7 copy-done.5
  11.0 37.7 %fetch_rows.1 = (bf16[256,512]{1,0:T(8,128)(2,1)S(1)}, s32[8,1024]{1,0:T(8,128)S(1)}, s32[8,256]{1,0:T(8,128)S(1)}, s32[8,128]{1,0:T(8,128)S(1)}) custom-call(s32[256,1]{1,0:T(8,128)S(1)} %copy.11.owner_ref, s32[1,256]{1,0:T(1,128)S(1)} %copy-done.4, s32[1,256]{1,0:T(1,128)S(1)} %copy-done.5, bf16[2048,512]{1,0:T(8,128)(2,1)S(1)} %copy-done), custom_call_target="tpu_custom_call" | custom-call | tf_op jit(solution)/shard_map/fetch_rows/pallas_call | solution.py:193
  48.7 0.0 copy-start.2
  48.7 0.7 copy-done.2
  49.4 0.0 copy-start.3
  49.4 0.6 copy-done.3
  50.0 40.9 %layer.1 = (bf16[256,512]{1,0:T(8,128)(2,1)}, bf16[256,512]{1,0:T(8,128)(2,1)}, f32[512,1024]{1,0:T(8,128)}, f32[256,512]{1,0:T(8,128)}) custom-call(bf16[256,512]{1,0:T(8,128)(2,1)} %copy-done.2, s32[8,128]{1,0:T(8,128)} %copy-done.3, bf16[512,1024]{1,0:T(8,128)(2,1)} %w_in_ref.1, bf16[256,512]{1,0:T(8,128)(2,1)} %w_out_ref.1, bf16[256,512]{1,0:T(8,128)(2,1)} %bitcast.3), custom_call_target="tpu_custom_call" | custom-call | tf_op jit(solution)/shard_map/layer/pallas_call | solution.py:520
  90.9 0.0 copy-start.1
  90.9 0.0 all-reduce.3.cloned.1.call-update
  91.0 0.9 copy-done.1
  91.9 41.0 %return_grads.1.landed_ref = bf16[1024,512]{1,0:T(8,128)(2,1)S(1)} custom-call(s32[8,256]{1,0:T(8,128)S(1)} %get-tuple-element.16.slot_ref, bf16[256,512]{1,0:T(8,128)(2,1)S(1)} %copy-done.1), custom_call_target="tpu_custom_call" | custom-call | tf_op jit(solution)/shard_map/return_grads/pallas_call | solution.py:610
  132.9 0.0 copy-start.7
  132.9 5.4 %scatter_rows.1 = f32[2048,512]{1,0:T(8,128)} custom-call(s32[8,1024]{1,0:T(8,128)S(1)} %get-tuple-element.15.want_ref, bf16[1024,512]{1,0:T(8,128)(2,1)S(1)} %return_grads.1.landed_ref), custom_call_target="tpu_custom_call" | custom-call | tf_op jit(solution)/shard_map/scatter_rows/pallas_call | solution.py:635
  138.3 131.5 %all-reduce.3.cloned.1.call-done = (f32[512,1024]{1,0:T(8,128)}, f32[256,512]{1,0:T(8,128)}) async-done(((f32[512,1024]{1,0:T(8,128)}, f32[256,512]{1,0:T(8,128)}), (f32[512,1024]{1,0:T(8,128)}, f32[256,512]{1,0:T(8,128)})) %all-reduce.3.cloned.1.call-update) | async-done | bytes 2621456 | tf_op jit(solution)/shard_map/psum | solution.py:656
  269.8 0.0 copy-done.7
  269.8 0.7 copy.17
  270.5 0.0 copy-start.6
  270.5 3.2 %copy.18 = f32[512,1024]{1,0:T(8,128)} copy(f32[512,1024]{1,0:T(8,128)} %get-tuple-element.28) | data formatting | bytes 4194304
  273.8 0.0 copy-done.6
  273.8 0.8 copy.19
Async XLA Ops:
  7.2 262.7 %all-reduce.3.cloned.1.call-start = ((), (), s32[]{:S(2)}) async-start(), calls=%async_computation | async-start | bytes 5242880 | tf_op jit(solution)/shard_map/psum | solution.py:656
  8.0 1.6 copy-start
  9.6 0.7 copy-start.4
  10.3 0.7 copy-start.5
  48.7 0.7 copy-start.2
  49.4 0.6 copy-start.3
  90.9 1.0 copy-start.1
  132.9 136.9 %copy-start.7 = (bf16[256,512]{1,0:T(8,128)(2,1)S(1)}, bf16[256,512]{1,0:T(8,128)(2,1)}, u32[]{:S(2)}) copy-start(bf16[256,512]{1,0:T(8,128)(2,1)} %get-tuple-element.14) | copy-start | bytes 786436
  270.5 3.2 %copy-start.6 = (f32[256,512]{1,0:T(8,128)S(1)}, f32[256,512]{1,0:T(8,128)}, u32[]{:S(2)}) copy-start(f32[256,512]{1,0:T(8,128)} %get-tuple-element.29) | copy-start | bytes 1572868
Sparse Core Ops, SparseCore 0:
  91.1 178.6 all-reduce.2

commit v3 on v2

v3 whole, which is shorter than its diff:
```python
import functools
import types

import jax
import jax.numpy as jnp
from jax import lax
from jax.experimental import pallas as pl
from jax.experimental.pallas import tpu as pltpu
from jax.sharding import PartitionSpec as P

MESH = pl.DeviceIdType.MESH
BF = jnp.bfloat16
F32 = jnp.float32
TOK = 256
WIDTH = 512
CAP = 8
ROWS = 2048
NB = 16
NG = 8
DEV = NB * NG
SLOTS = DEV * CAP


def iota(shape, dim):
    return lax.broadcasted_iota(jnp.int32, shape, dim)


def hot(mask):
    return jnp.where(mask, 1.0, 0.0).astype(BF)


def dot(a, b):
    return jnp.dot(a, b, preferred_element_type=F32)


def dot_t(a, b):
    return lax.dot_general(a, b, (((1,), (1,)), ((), ())), preferred_element_type=F32)


def column_of(line):
    size = line.shape[1]
    eye = iota((size, size), 0) == iota((size, size), 1)
    return jnp.sum(jnp.where(eye, line, 0.0), axis=1, keepdims=True)


def line_of(column):
    size = column.shape[0]
    eye = iota((size, size), 0) == iota((size, size), 1)
    return jnp.sum(jnp.where(eye, column, 0.0), axis=0, keepdims=True)


def device(p):
    return (p // NG, lax.rem(p, NG))


def greet_all(me):
    barrier = pltpu.get_barrier_semaphore()

    def greet(k, carry):
        pl.semaphore_signal(
            barrier, inc=1, device_id=device(lax.rem(me + k, DEV)), device_id_type=MESH
        )
        return carry

    lax.fori_loop(1, DEV, greet, 0)
    return barrier


def paired_halves(rows):
    count = rows.shape[0] // CAP
    split = rows.reshape(count, CAP, WIDTH)
    joined = jnp.concatenate([split[:, :, : WIDTH // 2], split[:, :, WIDTH // 2 :]], axis=1)
    return joined.reshape(count * 2 * CAP, WIDTH // 2).astype(BF)


def wait_bytes(view, sem):
    pltpu.make_async_copy(view, view, sem).wait()


HEADS = 4
DH = 64
HD = HEADS * DH
GROUP = TOK * NB
NORM_EPS = 1e-06
SPAN = 3
ATT = F32


def dot_rows(a, b):
    return lax.dot_general(a, b, (((0,), (0,)), ((), ())), preferred_element_type=F32)


def fold(rows):
    half = rows.shape[0] // 2
    return jnp.concatenate([rows[:half], rows[half:]], axis=1)


def unfold(rows):
    return jnp.concatenate([rows[:, :DH], rows[:, DH:]], axis=0)


def normalise(values):
    centred = values - jnp.mean(values, axis=-1, keepdims=True)
    scale = lax.rsqrt(jnp.mean(centred * centred, axis=-1, keepdims=True) + NORM_EPS)
    return centred * scale, scale


def norm_grad(grad, normed, scale):
    along = jnp.mean(grad * normed, axis=-1, keepdims=True)
    return scale * (grad - jnp.mean(grad, axis=-1, keepdims=True) - normed * along)


def tile(i, size=TOK):
    return pl.ds(pl.multiple_of(i * size, size), size)


def fetch_rows(r, me, b, g, barrier):
    owner = r.owner[...]
    owner_f = owner.astype(F32)
    lanes = iota((TOK, 128), 1)
    named = jnp.where(owner == lanes, 1.0, 0.0)
    before = hot(iota((TOK, TOK), 0) > iota((TOK, TOK), 1))
    rank = jnp.sum(dot(before, named.astype(BF)) * named, axis=1, keepdims=True)
    slot = owner_f * CAP + rank
    r.slot[...] = jnp.broadcast_to(line_of(slot), (8, TOK)).astype(jnp.int32)
    ask = column_of(r.row[...].astype(F32)) + 1.0
    high = jnp.floor(ask * (1.0 / 64.0))
    low = ask - 64.0 * high
    mine = rank.astype(jnp.int32) == lanes // 16
    named_t = hot(line_of(owner_f).astype(jnp.int32) == iota((DEV, TOK), 0))
    r.asked[...] = (
        64.0 * dot(named_t, jnp.where(mine, high, 0.0).astype(BF))
        + dot(named_t, jnp.where(mine, low, 0.0).astype(BF))
    ).astype(jnp.int32).reshape(DEV, 1, 128)
    seg = column_of(r.seg[...].astype(F32)).astype(jnp.int32)
    below = jnp.sum(jnp.where(seg < lanes, 1.0, 0.0), axis=0, keepdims=True)
    r.count_out[...] = jnp.broadcast_to(below, (8, 128))
    r.count_in[b] = jnp.broadcast_to(below, (8, 128))
    own = pltpu.make_async_copy(r.asked.at[me], r.asks.at[me], r.sems.at[1])
    own.start()
    own.wait()
    pl.semaphore_wait(barrier, DEV - 1)

    def ask_for(k, carry):
        p = lax.rem(me + k, DEV)
        pltpu.make_async_remote_copy(
            src_ref=r.asked.at[p], dst_ref=r.asks.at[me], send_sem=r.sems.at[2],
            recv_sem=r.sems.at[3], device_id=device(p), device_id_type=MESH,
        ).start()
        return carry

    lax.fori_loop(1, DEV, ask_for, 0)
    tallies = []
    for k in range(1, NB):
        tally = pltpu.make_async_remote_copy(
            src_ref=r.count_out, dst_ref=r.count_in.at[b], send_sem=r.count_send.at[k],
            recv_sem=r.count_recv.at[k], device_id=(lax.rem(b + k, NB), g), device_id_type=MESH,
        )
        tally.start()
        tallies.append(tally)
    for k, (source, into) in enumerate(r.loads):
        pltpu.make_async_copy(source, into, r.load_sems.at[k]).wait()
    wait_bytes(r.asks.at[pl.ds(0, DEV - 1)], r.sems.at[3])
    got = r.asks[...].reshape(DEV, 128).astype(F32)
    got_high = jnp.floor(got * (1.0 / 64.0))
    got_low = got - 64.0 * got_high
    spread = hot(iota((SLOTS, DEV), 0) // CAP == iota((SLOTS, DEV), 1))
    every = 64.0 * dot(spread, got_high.astype(BF)) + dot(spread, got_low.astype(BF))
    pick = lax.rem(iota((SLOTS, 128), 0), CAP) * 16 == iota((SLOTS, 128), 1)
    want = jnp.sum(jnp.where(pick, every, 0.0), axis=1, keepdims=True) - 1.0
    want = jnp.broadcast_to(want, (SLOTS, 128))
    r.want_v[...] = want.astype(jnp.int32)

    def rows_of(first, count):
        rows = r.want_v[pl.ds(first, count), :]
        return dot(hot(rows[:, :1] == iota((count, ROWS), 1)), r.table_v[...])

    exchange_rows(me, rows_of, r.rows_out, r.rows_in, r.sems.at[4], r.sems.at[5], r.sems.at[1])
    r.want[...] = want.T[:8].astype(jnp.int32)
    for tally in tallies:
        tally.wait()
    total = jnp.sum(r.count_in[...], axis=0)
    r.start[...] = total.astype(jnp.int32)
    slot = slot.astype(jnp.int32)
    place = (slot // CAP) * 16 + lax.rem(slot, CAP)
    spots = iota((TOK, 2 * SLOTS), 1)
    left, right = hot(place == spots), hot(place + CAP == spots)
    wait_bytes(r.rows_in.at[pl.ds(0, 16 * (DEV - 1))], r.sems.at[5])
    r.emb[:, : WIDTH // 2] = dot(left, r.rows_in[...]).astype(BF)
    r.emb[:, WIDTH // 2 :] = dot(right, r.rows_in[...]).astype(BF)


def exchange_rows(me, rows_of, out, into, send, recv, local):
    part = SLOTS // 4
    peers = DEV // 4

    def serve(i, carry):
        c = lax.rem(me // peers + i, 4)
        found = paired_halves(rows_of(pl.multiple_of(c * part, part), part))
        out[pl.ds(pl.multiple_of(c * 2 * part, 2 * part), 2 * part), :] = found

        def give(k, inner):
            p = c * peers + lax.rem(me + k, peers)

            @pl.when(p != me)
            def _():
                pltpu.make_async_remote_copy(
                    src_ref=out.at[pl.ds(pl.multiple_of(p * 16, 16), 16)],
                    dst_ref=into.at[pl.ds(pl.multiple_of(me * 16, 16), 16)],
                    send_sem=send, recv_sem=recv, device_id=device(p), device_id_type=MESH,
                ).start()

            return inner

        return lax.fori_loop(0, peers, give, carry)

    lax.fori_loop(0, 4, serve, 0)
    home = pl.ds(pl.multiple_of(me * 16, 16), 16)
    own = pltpu.make_async_copy(out.at[home], into.at[home], local)
    own.start()
    own.wait()


class Reduction:
    def __init__(self, r, which, width, part, core_in, held, first_in, second_in, last_in, full):
        self.r, self.which, self.width = r, which, width
        self.part, self.core_in, self.held = part, core_in, held
        self.first_in, self.second_in, self.last_in, self.full = (
            first_in, second_in, last_in, full,
        )
        b, g = lax.axis_index("bal"), lax.axis_index("grp")
        self.core = lax.rem(g, 2)
        y, x, z = g // 2, lax.rem(b, HEADS), b // HEADS
        self.twin = (b, g + 1 - 2 * self.core)
        self.axes = (
            (y, lambda p: (b, p * 2 + self.core)),
            (x, lambda p: (z * HEADS + p, g)),
            (z, lambda p: (p * HEADS + x, g)),
        )

    def columns(self, half):
        return pl.ds(half * self.width // 2, self.width // 2)

    def order(self, half):
        return (self.axes[half], self.axes[1 - half], self.axes[2])

    def copies(self, phase, half, axis, src, dst):
        here, device_of = axis
        out = []
        for k in range(1, HEADS):
            p = lax.rem(here + k, HEADS)
            out.append(
                pltpu.make_async_remote_copy(
                    src_ref=src(p), dst_ref=dst(here),
                    send_sem=self.r.red_send.at[self.which, phase, half, p],
                    recv_sem=self.r.red_recv.at[self.which, phase, half, here],
                    device_id=device_of(p), device_id_type=MESH,
                )
            )
        return out

    def views(self, phase, half):
        first, second, last = self.order(half)
        columns = self.columns(half)
        base = self.core * TOK
        if phase == 0:
            return (
                first,
                lambda p: self.held.at[pl.ds(pl.multiple_of(p * 64, 64), 64), columns],
                lambda p: self.first_in.at[half, p],
            )
        if phase == 1:
            return (
                second,
                lambda p: self.first_in.at[half, first[0], pl.ds(pl.multiple_of(p * 16, 16), 16)],
                lambda p: self.second_in.at[half, p],
            )
        if phase == 2:
            return (
                last,
                lambda p: self.last_in.at[half, last[0]],
                lambda p: self.last_in.at[half, p],
            )
        if phase == 3:
            def piece(p):
                row = pl.multiple_of(base + first[0] * 64 + p * 16, 16)
                return self.full.at[pl.ds(row, 16), columns]

            return second, lambda p: piece(second[0]), piece

        def block(p):
            return self.full.at[pl.ds(pl.multiple_of(base + p * 64, 64), 64), columns]

        return first, lambda p: block(first[0]), block

    def start(self, phase):
        for half in (0, 1):
            for copy in self.copies(phase, half, *self.views(phase, half)):
                copy.start()

    def take(self, phase, half):
        axis, src, dst = self.views(phase, half)
        here, device_of = axis
        for k in range(1, HEADS):
            p = lax.rem(here + k, HEADS)
            pltpu.make_async_remote_copy(
                src_ref=src(p), dst_ref=dst(p),
                send_sem=self.r.red_send.at[self.which, phase, half, p],
                recv_sem=self.r.red_recv.at[self.which, phase, half, p],
                device_id=device_of(p), device_id_type=MESH,
            ).wait_recv()

    def core_copy(self, back):
        rows = pl.ds(pl.multiple_of((1 - self.core) * TOK, TOK), TOK)
        if back:
            rows = pl.ds(pl.multiple_of(self.core * TOK, TOK), TOK)
        return pltpu.make_async_remote_copy(
            src_ref=(self.full if back else self.part).at[rows],
            dst_ref=self.full.at[rows] if back else self.core_in,
            send_sem=self.r.twin_send.at[self.which, back],
            recv_sem=self.r.twin_recv.at[self.which, back],
            device_id=self.twin, device_id_type=MESH,
        )

    def step(self, number):
        if number == 0:
            self.core_copy(0).start()
        elif number == 1:
            self.core_copy(0).wait_recv()
            rows = pl.ds(pl.multiple_of(self.core * TOK, TOK), TOK)
            self.held[...] = (
                self.part[rows, :].astype(F32) + self.core_in[...].astype(F32)
            ).astype(BF)
            self.start(0)
        elif number == 2:
            for half in (0, 1):
                here = self.order(half)[0][0]
                own = self.held[pl.ds(pl.multiple_of(here * 64, 64), 64), self.columns(half)]
                self.first_in[half, here] = own
                self.take(0, half)
                total = self.first_in[half, 0].astype(F32)
                for p in range(1, HEADS):
                    total += self.first_in[half, p].astype(F32)
                self.first_in[half, here] = total.astype(BF)
            self.start(1)
        elif number == 3:
            for half in (0, 1):
                first, second, last = self.order(half)
                rows = pl.ds(pl.multiple_of(second[0] * 16, 16), 16)
                self.second_in[half, second[0]] = self.first_in[half, first[0], rows]
                self.take(1, half)
                total = self.second_in[half, 0].astype(F32)
                for p in range(1, HEADS):
                    total += self.second_in[half, p].astype(F32)
                self.last_in[half, last[0]] = total.astype(BF)
            self.start(2)
        elif number == 4:
            for half in (0, 1):
                first, second, _ = self.order(half)
                self.take(2, half)
                total = self.last_in[half, 0].astype(F32)
                for p in range(1, HEADS):
                    total += self.last_in[half, p].astype(F32)
                row = pl.multiple_of(self.core * TOK + first[0] * 64 + second[0] * 16, 16)
                self.full[pl.ds(row, 16), self.columns(half)] = total.astype(BF)
            self.start(3)
        elif number == 5:
            for half in (0, 1):
                self.take(3, half)
            self.start(4)
        elif number == 6:
            for half in (0, 1):
                self.take(4, half)
            self.core_copy(1).start()
        else:
            rows = pl.ds(pl.multiple_of((1 - self.core) * TOK, TOK), TOK)
            pltpu.make_async_remote_copy(
                src_ref=self.full.at[rows], dst_ref=self.full.at[rows],
                send_sem=self.r.twin_send.at[self.which, 1],
                recv_sem=self.r.twin_recv.at[self.which, 1],
                device_id=self.twin, device_id_type=MESH,
            ).wait_recv()

    def finish(self):
        for back in (0, 1):
            self.core_copy(back).wait_send()
        for phase in range(5):
            for half in (0, 1):
                for copy in self.copies(phase, half, *self.views(phase, half)):
                    copy.wait_send()


def whole_kernel(names, *refs):
    r = types.SimpleNamespace(**dict(zip(names, refs)))
    b, g = lax.axis_index("bal"), lax.axis_index("grp")
    me = b * NG + g
    barrier = greet_all(me)
    r.loads = (
        (r.table_hbm, r.table_v), (r.w_in_hbm, r.w_in), (r.w_out_hbm, r.w_out), (r.cot_hbm, r.cot),
    )
    for k, (source, into) in enumerate(r.loads):
        pltpu.make_async_copy(source, into, r.load_sems.at[k]).start()
    fetch_rows(r, me, b, g, barrier)
    early = Reduction(
        r, 0, WIDTH, r.early_part, r.early_core, r.early_held, r.early_first, r.early_second,
        r.early_last, r.early_full,
    )
    late = Reduction(
        r, 1, 3 * HD, r.late_part, r.late_core, r.late_held, r.late_first, r.late_second,
        r.late_last, r.late_full,
    )
    z, x = b // HEADS, lax.rem(b, HEADS)
    def remote(src, dst, send, recv, at_z, at_x):
        return pltpu.make_async_remote_copy(
            src_ref=src, dst_ref=dst, send_sem=send, recv_sem=recv,
            device_id=(at_z * HEADS + at_x, g), device_id_type=MESH,
        )

    def spread(out, into, send, recv):
        for h in range(HEADS):
            @pl.when(h != x)
            def _():
                remote(out.at[h], into.at[x], send.at[h], recv.at[x], z, h).start()

            @pl.when(h == x)
            def _():
                into[h] = out[h]

    def collect(out, into, send, recv):
        for h in range(HEADS):
            @pl.when(h != x)
            def _():
                remote(out.at[h], into.at[h], send.at[h], recv.at[h], z, h).wait_recv()

    def sent(out, into, send, recv):
        for h in range(HEADS):
            @pl.when(h != x)
            def _():
                remote(out.at[h], into.at[h], send.at[h], recv.at[h], z, h).wait_send()

    embedded = r.emb[...].astype(F32)
    normed, _ = normalise(embedded)
    normed = normed.astype(BF)
    pre = dot(normed, r.w_in[...])
    sig = jax.nn.sigmoid(pre)
    act = pre * sig
    r.gate_v[...] = act[:, :HD].astype(BF)
    for h in range(HEADS):
        value, query, key = (
            act[:, part * HD + h * DH : part * HD + (h + 1) * DH] for part in (1, 2, 3)
        )
        r.kv_out[h] = jnp.concatenate([key, value], axis=1).astype(BF)
        r.q_out[h] = fold(query * 0.5).astype(BF)
    spread(r.q_out, r.q_in, r.q_send, r.q_recv)
    for dz in range(SPAN):
        for h in range(HEADS):
            @pl.when((z + dz < HEADS) & ((h != x) | (dz > 0)))
            def _():
                remote(
                    r.kv_out.at[h], r.kv_in.at[dz, x], r.kv_send.at[dz, h], r.kv_recv.at[dz, x], z + dz, h
                ).start()

            if dz == 0:
                @pl.when(h == x)
                def _():
                    r.kv_in[0, h] = r.kv_out[h]

    r.slope_v[...] = sig * (1.0 + pre * (1.0 - sig))
    r.att_v[...] = jnp.zeros_like(r.att_v)
    r.dq_v[...] = jnp.zeros_like(r.dq_v)
    places = z * HEADS * TOK + iota((HEADS * TOK, 128), 0)
    starts = r.start[:1, :]
    begin = jnp.max(jnp.where(starts <= places, starts, 0).astype(F32), axis=1, keepdims=True)
    r.begin_v[...] = jnp.broadcast_to(begin, (HEADS * TOK, 128)).astype(jnp.int32)
    collect(r.q_out, r.q_in, r.q_send, r.q_recv)
    for h in range(HEADS):
        q = unfold(r.q_in[h].astype(F32))
        r.q_v[h * TOK : (h + 1) * TOK, :] = jnp.concatenate(
            [q, jnp.zeros((TOK, DH), F32)], axis=1
        ).astype(BF)
        r.qt_v[:, h * TOK : (h + 1) * TOK] = q.T.astype(BF)

    def forward_pair(dz, i, j):
        kv = r.kv_in[dz, j]
        scores = dot_t(r.q_v[tile(i), :], kv)
        half = jnp.tanh(scores)
        more = 1.0 + half
        key_pos = ((z - dz) * HEADS + j) * TOK + iota((TOK, TOK), 1)
        visible = key_pos >= r.begin_v[tile(i), :1]
        if dz == 0:
            visible &= key_pos <= (z * HEADS + i) * TOK + iota((TOK, TOK), 0)
        weight = jnp.where(visible, scores * more, 0.0).astype(BF)
        r.w_v[dz, i * HEADS + j] = weight
        r.s_v[dz, i * HEADS + j] = jnp.where(
            visible, more * (1.0 + scores * (1.0 - half)), 0.0
        ).astype(BF)
        r.att_v[tile(i), :] += dot(weight, kv)

    def arrived(dz):
        for h in range(HEADS):
            def arrival():
                remote(
                    r.kv_out.at[h], r.kv_in.at[dz, h], r.kv_send.at[dz, h], r.kv_recv.at[dz, h], z, h
                ).wait_recv()

            if dz == 0:
                pl.when(h != x)(arrival)
            else:
                arrival()

    def sweep(body, dz):
        def outer(i, carry):
            low = 0 if dz < 2 else i
            high = i + 1 if dz == 0 else HEADS

            def inner(j, carry):
                body(dz, i, j)
                return carry

            return lax.fori_loop(low, high, inner, carry)

        lax.fori_loop(0, HEADS, outer, 0)

    for dz in range(SPAN):
        @pl.when(z >= dz)
        def _():
            arrived(dz)
            sweep(forward_pair, dz)

    for h in range(HEADS):
        att = r.att_v[h * TOK : (h + 1) * TOK, DH:] * (2.0 / GROUP)
        r.att_out[h] = fold(att).astype(ATT)
    spread(r.att_out, r.att_in, r.a_send, r.a_recv)
    cot = r.cot[...]
    d_mixed = dot_t(cot, r.w_out[...])
    gate = r.gate_v[...].astype(F32)
    collect(r.att_out, r.att_in, r.a_send, r.a_recv)

    attended = jnp.concatenate([unfold(r.att_in[h].astype(F32)) for h in range(HEADS)], axis=1)
    level, scale = normalise(attended)
    delta = norm_grad(d_mixed * gate, level, scale)
    for h in range(HEADS):
        r.d_out[h] = fold(delta[:, h * DH : (h + 1) * DH]).astype(BF)
    spread(r.d_out, r.d_in, r.d_send, r.d_recv)
    mixed = (level * gate).astype(BF)
    r.layer_out[...] = (dot(mixed, r.w_out[...]) + r.emb[...].astype(F32)).astype(BF)
    d_gate = (d_mixed * level).astype(BF).astype(F32)
    r.joined[:, :HD] = (d_gate * r.slope_v[:, :HD]).astype(BF)
    embedded = r.emb[...].astype(F32)
    normed = normalise(embedded)[0].astype(BF)
    r.early_part[:, :HD] = dot_rows(normed, r.joined[:, :HD]).astype(BF)
    out_grad = dot_rows(mixed, cot)
    r.early_part[:HD, HD:] = out_grad[:, : WIDTH // 2].astype(BF)
    r.early_part[HD:, HD:] = out_grad[:, WIDTH // 2 :].astype(BF)
    early.step(0)
    collect(r.d_out, r.d_in, r.d_send, r.d_recv)
    for h in range(HEADS):
        d = unfold(r.d_in[h].astype(F32))
        r.q_v[HEADS * TOK + h * TOK : HEADS * TOK + (h + 1) * TOK, :] = jnp.concatenate(
            [jnp.zeros((TOK, DH), F32), d], axis=1
        ).astype(BF)
        r.dt_v[:, h * TOK : (h + 1) * TOK] = d.T.astype(BF)

    def backward(dz):
        def keys(j, carry):
            kv = r.kv_in[dz, j]

            def queries(i, grads):
                dk, dv = grads
                product = dot_t(r.q_v[tile(HEADS + i), :], kv)
                d_score = (product * r.s_v[dz, i * HEADS + j].astype(F32)).astype(BF)
                r.dq_v[tile(i), :] += dot(d_score, kv)
                dk = dk + dot(r.qt_v[:, tile(i)], d_score)
                dv = dv + dot(r.dt_v[:, tile(i)], r.w_v[dz, i * HEADS + j])
                return dk, dv

            low = j if dz == 0 else 0
            high = j + 1 if dz == 2 else HEADS
            zeros = jnp.zeros((DH, TOK), F32)
            dk, dv = lax.fori_loop(low, high, queries, (zeros, zeros))
            grads = jnp.concatenate([dk, dv], axis=0) * (2.0 / GROUP)
            r.g_out[dz, j] = grads.T.astype(BF)
            if dz == 0:
                @pl.when(j != x)
                def _():
                    remote(
                        r.g_out.at[0, j], r.g_in.at[0, x], r.g_send.at[0, j], r.g_recv.at[0, x], z, j
                    ).start()

                @pl.when(j == x)
                def _():
                    r.g_in[0, j] = r.g_out[0, j]
            else:
                remote(
                    r.g_out.at[dz, j], r.g_in.at[dz, x], r.g_send.at[dz, j], r.g_recv.at[dz, x], z - dz, j
                ).start()
            return carry

        lax.fori_loop(0, HEADS, keys, 0)

    for dz in reversed(range(SPAN)):
        @pl.when(z >= dz)
        def _():
            backward(dz)

        early.step(SPAN - dz)

    for h in range(HEADS):
        r.dq_out[h] = fold(r.dq_v[h * TOK : (h + 1) * TOK, :DH] * (1.0 / GROUP)).astype(BF)
    spread(r.dq_out, r.dq_in, r.e_send, r.e_recv)

    spread_in, spread_scale = normalise(embedded)
    normed = spread_in.astype(BF)
    for dz in reversed(range(SPAN)):
        for h in range(HEADS):
            def arrival():
                remote(
                    r.g_out.at[dz, h], r.g_in.at[dz, h], r.g_send.at[dz, h], r.g_recv.at[dz, h], z, h
                ).wait_recv()

            if dz == 0:
                pl.when(h != x)(arrival)
            else:
                pl.when(z + dz < HEADS)(arrival)

    collect(r.dq_out, r.dq_in, r.e_send, r.e_recv)
    for h in range(HEADS):
        total = r.g_in[0, h].astype(F32)
        for dz in range(1, SPAN):
            total += jnp.where(z + dz < HEADS, r.g_in[dz, h].astype(F32), 0.0)
        r.joined[:, HD + h * DH : HD + (h + 1) * DH] = total[:, DH:].astype(BF)
        r.joined[:, 2 * HD + h * DH : 2 * HD + (h + 1) * DH] = unfold(
            r.dq_in[h].astype(F32)
        ).astype(BF)
        r.joined[:, 3 * HD + h * DH : 3 * HD + (h + 1) * DH] = total[:, :DH].astype(BF)
    r.joined[:, HD:] = (r.joined[:, HD:].astype(F32) * r.slope_v[:, HD:]).astype(BF)
    r.late_part[...] = dot_rows(normed, r.joined[:, HD:]).astype(BF)
    late.step(0)
    early.step(4)
    d_normed = dot_t(r.joined[...], r.w_in[...])
    r.demb[...] = (
        norm_grad(d_normed, spread_in, spread_scale) + r.cot[...].astype(F32)
    ).astype(BF)

    def grads_of(first, count):
        return dot(hot(r.slot[:1, :] == iota((count, TOK), 0) + first), r.demb[...])

    exchange_rows(me, grads_of, r.grads_out, r.grads_in, r.sems.at[6], r.sems.at[7], r.sems.at[1])
    late.step(1)
    early.step(5)
    late.step(2)
    early.step(6)
    late.step(3)
    early.step(7)
    r.early[...] = r.early_full[...]
    for number in range(4, 8):
        late.step(number)
    r.late[...] = r.late_full[...]
    wait_bytes(r.grads_in.at[pl.ds(0, 16 * (DEV - 1))], r.sems.at[7])
    halves = r.grads_in[...].astype(F32).reshape(DEV, 2 * CAP, WIDTH // 2)
    whole = jnp.concatenate([halves[:, :CAP], halves[:, CAP:]], axis=2)
    r.landed[...] = whole.reshape(SLOTS, WIDTH).astype(BF)

    sent(r.q_out, r.q_in, r.q_send, r.q_recv)
    sent(r.att_out, r.att_in, r.a_send, r.a_recv)
    sent(r.d_out, r.d_in, r.d_send, r.d_recv)
    sent(r.dq_out, r.dq_in, r.e_send, r.e_recv)
    for dz in range(SPAN):
        for h in range(HEADS):
            @pl.when((z + dz < HEADS) & ((h != x) | (dz > 0)))
            def _():
                remote(
                    r.kv_out.at[h], r.kv_in.at[dz, h], r.kv_send.at[dz, h], r.kv_recv.at[dz, h], z, h
                ).wait_send()

            @pl.when((z >= dz) & ((h != x) | (dz > 0)))
            def _():
                remote(
                    r.g_out.at[dz, h], r.g_in.at[dz, h], r.g_send.at[dz, h], r.g_recv.at[dz, h], z, h
                ).wait_send()
    early.finish()
    late.finish()
    wait_bytes(r.asked.at[pl.ds(0, DEV - 1)], r.sems.at[2])
    wait_bytes(r.rows_out.at[pl.ds(0, 16 * (DEV - 1))], r.sems.at[4])
    wait_bytes(r.grads_out.at[pl.ds(0, 16 * (DEV - 1))], r.sems.at[6])


VMEM = pl.BlockSpec(memory_space=pltpu.VMEM)
ANY = pl.BlockSpec(memory_space=pl.ANY)


def whole(owner, row, seg, table, w_in, w_out, cot):
    dma = pltpu.SemaphoreType.DMA
    I32 = jnp.int32
    outs = dict(
        layer_out=((TOK, WIDTH), BF),
        want=((8, SLOTS), I32),
        landed=((SLOTS, WIDTH), BF),
        early=((WIDTH, WIDTH), BF),
        late=((WIDTH, 3 * HD), BF),
    )
    scratch = dict(
        table_v=((ROWS, WIDTH), BF),
        w_in=((WIDTH, 4 * HD), BF),
        w_out=((HD, WIDTH), BF),
        cot=((TOK, WIDTH), BF),
        emb=((TOK, WIDTH), BF),
        demb=((TOK, WIDTH), BF),
        slot=((8, TOK), I32),
        start=((8, 128), I32),
        asked=((DEV, 1, 128), I32),
        asks=((DEV, 1, 128), I32),
        want_v=((SLOTS, 128), I32),
        rows_out=((2 * SLOTS, WIDTH // 2), BF),
        rows_in=((2 * SLOTS, WIDTH // 2), BF),
        grads_out=((2 * SLOTS, WIDTH // 2), BF),
        grads_in=((2 * SLOTS, WIDTH // 2), BF),
        count_out=((8, 128), F32),
        count_in=((NB, 8, 128), F32),
        slope_v=((TOK, 4 * HD), F32),
        gate_v=((TOK, HD), BF),
        kv_out=((HEADS, TOK, 2 * DH), BF),
        q_out=((HEADS, TOK // 2, 2 * DH), BF),
        kv_in=((SPAN, HEADS, TOK, 2 * DH), BF),
        q_in=((HEADS, TOK // 2, 2 * DH), BF),
        q_v=((2 * HEADS * TOK, 2 * DH), BF),
        qt_v=((DH, HEADS * TOK), BF),
        begin_v=((HEADS * TOK, 128), I32),
        w_v=((SPAN, HEADS * HEADS, TOK, TOK), BF),
        s_v=((SPAN, HEADS * HEADS, TOK, TOK), BF),
        att_v=((HEADS * TOK, 2 * DH), F32),
        att_out=((HEADS, TOK // 2, 2 * DH), ATT),
        att_in=((HEADS, TOK // 2, 2 * DH), ATT),
        d_out=((HEADS, TOK // 2, 2 * DH), BF),
        d_in=((HEADS, TOK // 2, 2 * DH), BF),
        dt_v=((DH, HEADS * TOK), BF),
        dq_v=((HEADS * TOK, 2 * DH), F32),
        dq_out=((HEADS, TOK // 2, 2 * DH), BF),
        dq_in=((HEADS, TOK // 2, 2 * DH), BF),
        g_out=((SPAN, HEADS, TOK, 2 * DH), BF),
        g_in=((SPAN, HEADS, TOK, 2 * DH), BF),
        joined=((TOK, 4 * HD), BF),
    )
    for name, width in (("early", WIDTH), ("late", 3 * HD)):
        scratch |= {
            name + "_part": ((WIDTH, width), BF),
            name + "_core": ((TOK, width), BF),
            name + "_held": ((TOK, width), BF),
            name + "_first": ((2, HEADS, 64, width // 2), BF),
            name + "_second": ((2, HEADS, 16, width // 2), BF),
            name + "_last": ((2, HEADS, 16, width // 2), BF),
            name + "_full": ((WIDTH, width), BF),
        }
    sems = dict(
        sems=(8,), load_sems=(4,), count_send=(NB,), count_recv=(NB,),
        kv_send=(SPAN, HEADS), kv_recv=(SPAN, HEADS), q_send=(HEADS,), q_recv=(HEADS,),
        a_send=(HEADS,), a_recv=(HEADS,), d_send=(HEADS,), d_recv=(HEADS,),
        g_send=(SPAN, HEADS), g_recv=(SPAN, HEADS), e_send=(HEADS,), e_recv=(HEADS,),
        red_send=(2, 5, 2, HEADS), red_recv=(2, 5, 2, HEADS), twin_send=(2, 2), twin_recv=(2, 2),
    )
    names = ["owner", "row", "seg", "table_hbm", "w_in_hbm", "w_out_hbm", "cot_hbm"]
    names += [*outs, *scratch, *sems]
    return pl.pallas_call(
        functools.partial(whole_kernel, names),
        out_shape=tuple(jax.ShapeDtypeStruct(*kind) for kind in outs.values()),
        in_specs=[VMEM] * 3 + [ANY] * 4,
        out_specs=(VMEM,) * len(outs),
        scratch_shapes=[pltpu.VMEM(*kind) for kind in scratch.values()]
        + [dma(shape) for shape in sems.values()],
        compiler_params=pltpu.CompilerParams(
            collective_id=0, has_side_effects=True, vmem_limit_bytes=58 << 20
        ),
        name="whole_layer",
    )(owner, row, seg, table, w_in, w_out, cot)


def scatter_kernel(want_ref, landed_ref, early_ref, late_ref, table_ref, w_in_ref, w_out_ref):
    part = table_ref.shape[0]
    rows = iota((part, SLOTS), 0) + pl.program_id(0) * part
    table_ref[...] = dot(hot(want_ref[:1, :] == rows), landed_ref[...])
    size = w_in_ref.shape[0]
    here = tile(pl.program_id(0), size)
    w_in_ref[:, :HD] = early_ref[here, :HD].astype(F32)
    w_in_ref[:, HD:] = late_ref[here, :].astype(F32)
    size = w_out_ref.shape[0]
    step = pl.program_id(0)
    w_out_ref[:, : WIDTH // 2] = early_ref[tile(step, size), HD:].astype(F32)
    below = pl.ds(pl.multiple_of(step * size + HD, size), size)
    w_out_ref[:, WIDTH // 2 :] = early_ref[below, HD:].astype(F32)


def scatter_add(want, landed, early, late):
    steps = 8
    still = lambda i: (0, 0)
    return pl.pallas_call(
        scatter_kernel,
        grid=(steps,),
        out_shape=(
            jax.ShapeDtypeStruct((ROWS, WIDTH), F32),
            jax.ShapeDtypeStruct((WIDTH, 4 * HD), F32),
            jax.ShapeDtypeStruct((HD, WIDTH), F32),
        ),
        in_specs=[
            pl.BlockSpec((8, SLOTS), still),
            pl.BlockSpec((SLOTS, WIDTH), still),
            pl.BlockSpec((WIDTH, WIDTH), still),
            pl.BlockSpec((WIDTH, 3 * HD), still),
        ],
        out_specs=(
            pl.BlockSpec((ROWS // steps, WIDTH), lambda i: (i, 0)),
            pl.BlockSpec((WIDTH // steps, 4 * HD), lambda i: (i, 0)),
            pl.BlockSpec((HD // steps, WIDTH), lambda i: (i, 0)),
        ),
        compiler_params=pltpu.CompilerParams(vmem_limit_bytes=32 << 20),
        name="scatter_rows",
    )(want, landed, early, late)


def per_device(table, item_owner, item_row, segment, w_in, w_out, cotangent):
    layer_out, want, landed, early, late = whole(
        item_owner[0], item_row, segment, table, w_in, w_out, cotangent[0]
    )
    table_grad, w_in_grad, w_out_grad = scatter_add(want, landed, early, late)
    return (layer_out[None], table_grad, w_in_grad, w_out_grad)


def solution(mesh):
    placed = (
        P(("bal", "grp"), None),
        P("grp", "bal", None),
        P("grp", "bal"),
        P("grp", "bal"),
        P(),
        P(),
        P("grp", "bal", None),
    )
    return jax.shard_map(
        per_device,
        mesh=mesh,
        in_specs=placed,
        out_specs=(P("grp", "bal", None), P(("bal", "grp"), None), P(), P()),
        check_vma=False,
    )
```

time: 282 us -> 143 us (0.51)
  waiting for transfers between devices: 132 us -> 0 us
  between operations: 14.1 us -> 0.65 us
  Pallas kernels: 125 us -> 135 us
  local copies, waits for them, and re-layouts: 10.7 us -> 6.33 us
    psum x1 -> x0, waiting for transfers between devices: 132 us -> none  [per_device(): w_in_grad, w_out_grad = lax.psum((w_in_part, w_out_part), ('bal', 'grp'))]
    pallas_call x4 -> x2, Pallas kernels: 125 us -> 135 us  [the longest x1 130 us: whole(): pl.pallas_call(functools.partial(whole_kernel, names), out_shape=tuple((j...]
    unnamed x19 -> x11, local copies, waits for them, and re-layouts: 9.87 us -> 4.86 us
  transfers between devices with their start and end apart: 1 -> 0, of which waited for: 1 -> 0; matrix products, arithmetic and copies ran while one was open for 0% -> 0% of each run, Pallas kernels for 16% -> 0%
where the time goes in v3:
time: 143 us; the launch traced here: 142 us
  Pallas kernels  135 us (94%)
  local copies, waits for them, and re-layouts  6.33 us (4%)
    pallas_call x1, Pallas kernels, whole(): pl.pallas_call(functools.partial(whole_kernel, names), out_shape=tuple((j...  130 us
    pallas_call x1, Pallas kernels, scatter_add(): pl.pallas_call(scatter_kernel, grid=(steps,), out_shape=(jax.ShapeDtypeSt...  5.37 us
    unnamed x11, local copies, waits for them, and re-layouts  4.86 us

profile of v3, /device:TPU:1, one launch (start us, length us, event | category | flops | bytes accessed | tf_op | source)
XLA Modules:
  0.0 142.4 jit_solution(14387710672034352930)
XLA Ops:
  0.6 1.5 %copy.11.refs_0_ = s32[256,1]{1,0:T(8,128)} copy(s32[256,1]{0,1:T(1,128)} %bitcast.5) | data formatting | bytes 2048 | tf_op jit(solution)/shard_map/squeeze | solution.py:821
  2.1 130.0 %whole_layer.1 = (bf16[256,512]{1,0:T(8,128)(2,1)}, s32[8,1024]{1,0:T(8,128)}, bf16[1024,512]{1,0:T(8,128)(2,1)}, bf16[512,512]{1,0:T(8,128)(2,1)}, bf16[512,768]{1,0:T(8,128)(2,1)}) custom-call(s32[256,1]{1,0:T(8,128)} %copy.11.refs_0_, s32[1,256]{1,0:T(1,128)} %refs_1_.1, s32[1,256]{1,0:T(1,128)} %refs_2_.1, bf16[2048,512]{1,0:T(8,128)(2,1)} %refs_3_.1, ...), custom_call_target="tpu_custom_call" | custom-call | tf_op jit(solution)/shard_map/whole_layer/pallas_call | solution.py:763
  132.2 0.0 copy-start
  132.2 1.2 copy-done
  133.4 0.0 copy-start.1
  133.4 1.1 copy-done.1
  134.5 0.0 copy-start.2
  134.5 1.0 copy-done.2
  135.6 0.0 copy-start.3
  135.6 0.8 copy-done.3
  136.3 0.0 copy-start.4
  136.3 5.4 %scatter_rows.1 = (f32[2048,512]{1,0:T(8,128)}, f32[512,1024]{1,0:T(8,128)}, f32[256,512]{1,0:T(8,128)}) custom-call(s32[8,1024]{1,0:T(8,128)S(1)} %copy-done.3, bf16[1024,512]{1,0:T(8,128)(2,1)S(1)} %copy-done, bf16[512,512]{1,0:T(8,128)(2,1)S(1)} %copy-done.2, bf16[512,768]{1,0:T(8,128)(2,1)S(1)} %copy-done.1), custom_call_target="tpu_custom_call" | custom-call | tf_op jit(solution)/shard_map/scatter_rows/pallas_call | solution.py:795
  141.7 0.0 copy-done.4
  141.7 0.7 copy.13
Async XLA Ops:
  132.2 1.2 copy-start
  133.4 1.1 copy-start.1
  134.5 1.0 copy-start.2
  135.6 0.8 copy-start.3
  136.3 5.4 %copy-start.4 = (bf16[256,512]{1,0:T(8,128)(2,1)S(1)}, bf16[256,512]{1,0:T(8,128)(2,1)}, u32[]{:S(2)}) copy-start(bf16[256,512]{1,0:T(8,128)(2,1)} %get-tuple-element.12) | copy-start | bytes 786436

commit v4 on v3

v4 whole, which is shorter than its diff:
```python
import functools
import types

import jax
import jax.numpy as jnp
from jax import lax
from jax.experimental import pallas as pl
from jax.experimental.pallas import tpu as pltpu
from jax.sharding import PartitionSpec as P

MESH = pl.DeviceIdType.MESH
BF = jnp.bfloat16
F32 = jnp.float32
TOK = 256
WIDTH = 512
CAP = 8
ROWS = 2048
NB = 16
NG = 8
DEV = NB * NG
SLOTS = DEV * CAP


def iota(shape, dim):
    return lax.broadcasted_iota(jnp.int32, shape, dim)


def hot(mask):
    return jnp.where(mask, 1.0, 0.0).astype(BF)


def dot(a, b):
    return jnp.dot(a, b, preferred_element_type=F32)


def dot_t(a, b):
    return lax.dot_general(a, b, (((1,), (1,)), ((), ())), preferred_element_type=F32)


def column_of(line):
    size = line.shape[1]
    eye = iota((size, size), 0) == iota((size, size), 1)
    return jnp.sum(jnp.where(eye, line, 0.0), axis=1, keepdims=True)


def line_of(column):
    size = column.shape[0]
    eye = iota((size, size), 0) == iota((size, size), 1)
    return jnp.sum(jnp.where(eye, column, 0.0), axis=0, keepdims=True)


def place_of(z, x, y, rest):
    return lax.rem(z + x + y, 4) * 32 + rest


def device(p):
    rest = lax.rem(p, 32)
    x, y = rest // 8, lax.rem(rest, 8) // 2
    z = lax.rem(p // 32 + 8 - x - y, 4)
    return (z * 4 + x, lax.rem(rest, NG))


def greet_all(me):
    barrier = pltpu.get_barrier_semaphore()

    def greet(k, carry):
        pl.semaphore_signal(
            barrier, inc=1, device_id=device(lax.rem(me + k, DEV)), device_id_type=MESH
        )
        return carry

    lax.fori_loop(1, DEV, greet, 0)
    return barrier


def paired_halves(rows):
    count = rows.shape[0] // CAP
    split = rows.reshape(count, CAP, WIDTH)
    joined = jnp.concatenate([split[:, :, : WIDTH // 2], split[:, :, WIDTH // 2 :]], axis=1)
    return joined.reshape(count * 2 * CAP, WIDTH // 2).astype(BF)


def wait_bytes(view, sem):
    pltpu.make_async_copy(view, view, sem).wait()


HEADS = 4
DH = 64
HD = HEADS * DH
GROUP = TOK * NB
NORM_EPS = 1e-06
SPAN = 3
ATT = F32


def dot_rows(a, b):
    return lax.dot_general(a, b, (((0,), (0,)), ((), ())), preferred_element_type=F32)


def fold(rows):
    half = rows.shape[0] // 2
    return jnp.concatenate([rows[:half], rows[half:]], axis=1)


def unfold(rows):
    return jnp.concatenate([rows[:, :DH], rows[:, DH:]], axis=0)


def normalise(values):
    centred = values - jnp.mean(values, axis=-1, keepdims=True)
    scale = lax.rsqrt(jnp.mean(centred * centred, axis=-1, keepdims=True) + NORM_EPS)
    return centred * scale, scale


def norm_grad(grad, normed, scale):
    along = jnp.mean(grad * normed, axis=-1, keepdims=True)
    return scale * (grad - jnp.mean(grad, axis=-1, keepdims=True) - normed * along)


def tile(i, size=TOK):
    if isinstance(i, int):
        return pl.ds(i * size, size)
    return pl.ds(pl.multiple_of(i * size, size), size)


def fetch_rows(r, me, b, g, barrier):
    owner_line = r.owner[...]
    rest = lax.rem(owner_line, 32)
    owner_line = place_of(owner_line // 32, rest // 8, lax.rem(rest, 8) // 2, rest)
    owner_f = column_of(owner_line.astype(F32))
    owner = owner_f.astype(jnp.int32)
    lanes = iota((TOK, 128), 1)
    named = jnp.where(owner == lanes, 1.0, 0.0)
    before = hot(iota((TOK, TOK), 0) > iota((TOK, TOK), 1))
    rank = jnp.sum(dot(before, named.astype(BF)) * named, axis=1, keepdims=True)
    slot = owner_f * CAP + rank
    r.slot[...] = jnp.broadcast_to(line_of(slot), (8, TOK)).astype(jnp.int32)
    ask = column_of(r.row[...].astype(F32)) + 1.0
    high = jnp.floor(ask * (1.0 / 64.0))
    low = ask - 64.0 * high
    mine = rank.astype(jnp.int32) == lanes // 16
    named_t = hot(owner_line == iota((DEV, TOK), 0))
    r.asked[...] = (
        64.0 * dot(named_t, jnp.where(mine, high, 0.0).astype(BF))
        + dot(named_t, jnp.where(mine, low, 0.0).astype(BF))
    ).astype(jnp.int32).reshape(DEV, 1, 128)
    seg = column_of(r.seg[...].astype(F32)).astype(jnp.int32)
    below = jnp.sum(jnp.where(seg < lanes, 1.0, 0.0), axis=0, keepdims=True)
    r.count_out[...] = jnp.broadcast_to(below, (8, 128))
    r.count_in[b] = jnp.broadcast_to(below, (8, 128))
    own = pltpu.make_async_copy(r.asked.at[me], r.asks.at[me], r.sems.at[1])
    own.start()
    own.wait()
    pl.semaphore_wait(barrier, DEV - 1)

    def ask_for(k, carry):
        p = lax.rem(me + k, DEV)
        pltpu.make_async_remote_copy(
            src_ref=r.asked.at[p], dst_ref=r.asks.at[me], send_sem=r.sems.at[2],
            recv_sem=r.sems.at[3], device_id=device(p), device_id_type=MESH,
        ).start()
        return carry

    lax.fori_loop(1, DEV, ask_for, 0)
    tallies = []
    for k in range(1, NB):
        tally = pltpu.make_async_remote_copy(
            src_ref=r.count_out, dst_ref=r.count_in.at[b], send_sem=r.count_send.at[k],
            recv_sem=r.count_recv.at[k], device_id=(lax.rem(b + k, NB), g), device_id_type=MESH,
        )
        tally.start()
        tallies.append(tally)
    for k, (source, into) in enumerate(r.loads):
        pltpu.make_async_copy(source, into, r.load_sems.at[k]).wait()
    wait_bytes(r.asks.at[pl.ds(0, DEV - 1)], r.sems.at[3])
    got = r.asks[...].reshape(DEV, 128).astype(F32)
    got_high = jnp.floor(got * (1.0 / 64.0))
    got_low = got - 64.0 * got_high
    spread = hot(iota((SLOTS, DEV), 0) // CAP == iota((SLOTS, DEV), 1))
    every = 64.0 * dot(spread, got_high.astype(BF)) + dot(spread, got_low.astype(BF))
    pick = lax.rem(iota((SLOTS, 128), 0), CAP) * 16 == iota((SLOTS, 128), 1)
    want = jnp.sum(jnp.where(pick, every, 0.0), axis=1, keepdims=True) - 1.0
    want = jnp.broadcast_to(want, (SLOTS, 128))
    r.want_v[...] = want.astype(jnp.int32)

    def rows_of(first, count):
        rows = r.want_v[pl.ds(first, count), :]
        return dot(hot(rows[:, :1] == iota((count, ROWS), 1)), r.table_v[...])

    rows = RowExchange(
        me, rows_of, r.rows_out, r.rows_in, r.sems.at[4], r.sems.at[5], r.sems.at[1]
    )
    for i in range(4):
        rows.serve(i)
    r.want_t[...] = want.T[:8].astype(jnp.int32)
    pltpu.make_async_copy(r.want_t, r.want, r.store_sems.at[0]).start()
    for tally in tallies:
        tally.wait()
    total = jnp.sum(r.count_in[...], axis=0)
    r.start[...] = total.astype(jnp.int32)
    slot = slot.astype(jnp.int32)
    place = (slot // CAP) * 16 + lax.rem(slot, CAP)
    spots = iota((TOK, 2 * SLOTS), 1)
    left, right = hot(place == spots), hot(place + CAP == spots)
    rows.take()
    r.emb[:, : WIDTH // 2] = dot(left, r.rows_in[...]).astype(BF)
    r.emb[:, WIDTH // 2 :] = dot(right, r.rows_in[...]).astype(BF)
    return rows


class RowExchange:
    def __init__(self, me, rows_of, out, into, send, recv, local):
        self.me, self.rows_of, self.out, self.into = me, rows_of, out, into
        self.send, self.recv, self.local = send, recv, local

    def serve(self, i):
        me, part, peers = self.me, SLOTS // 4, DEV // 4
        c = lax.rem(me // peers + i, 4)
        found = paired_halves(self.rows_of(pl.multiple_of(c * part, part), part))
        self.out[pl.ds(pl.multiple_of(c * 2 * part, 2 * part), 2 * part), :] = found

        def give(k, carry):
            p = c * peers + lax.rem(me + k, peers)
            pltpu.make_async_remote_copy(
                src_ref=self.out.at[pl.ds(pl.multiple_of(p * 16, 16), 16)],
                dst_ref=self.into.at[pl.ds(pl.multiple_of(me * 16, 16), 16)],
                send_sem=self.send, recv_sem=self.recv,
                device_id=device(p), device_id_type=MESH,
            ).start()
            return carry

        lax.fori_loop(1 if i == 0 else 0, peers, give, 0)
        if i == 0:
            home = pl.ds(pl.multiple_of(me * 16, 16), 16)
            own = pltpu.make_async_copy(self.out.at[home], self.into.at[home], self.local)
            own.start()
            own.wait()

    def take(self):
        wait_bytes(self.into.at[pl.ds(0, 16 * (DEV - 1))], self.recv)

    def finish(self):
        wait_bytes(self.out.at[pl.ds(0, 16 * (DEV - 1))], self.send)


class Reduction:
    def __init__(self, r, name):
        for kind in ("part", "held", "first", "second", "third", "full", "send", "recv"):
            setattr(self, kind, getattr(r, name + "_" + kind))
        b, g = lax.axis_index("bal"), lax.axis_index("grp")
        z, x, y, c = b // 4, lax.rem(b, 4), g // 2, lax.rem(g, 2)
        by_y = (g, lambda p: (b, p))
        by_x = (x * 2 + c, lambda p: (z * 4 + p // 2, y * 2 + lax.rem(p, 2)))
        only_y = (y, lambda p: (b, p * 2 + c))
        only_x = (x, lambda p: (z * 4 + p, g))
        only_z = (z, lambda p: (p * 4 + x, g))
        self.groups = ((by_y, only_x, only_z), (by_x, only_y, only_z))

    def give(self, unit, phase, group, src, dst):
        here, device_of = group
        count = NG if phase in (0, 4) else 4
        for k in range(1, count):
            p = lax.rem(here + k, count)
            pltpu.make_async_remote_copy(
                src_ref=src(p), dst_ref=dst(here),
                send_sem=self.send.at[unit, phase], recv_sem=self.recv.at[unit, phase],
                device_id=device_of(p), device_id_type=MESH,
            ).start()

    def view(self, unit, phase):
        if phase == 0:
            return self.first.at[unit, pl.ds(0, NG - 1)]
        if phase == 4:
            return self.full.at[unit, pl.ds(0, (NG - 1) * 64)]
        if phase == 3:
            return self.full.at[unit, pl.ds(0, 3 * 16)]
        return (self.second if phase == 1 else self.third).at[unit, pl.ds(0, 3)]

    def step(self, number):
        for unit in (0, 1):
            if number > 0:
                wait_bytes(self.view(unit, number - 1), self.recv.at[unit, number - 1])
            self.step_of(number, unit)

    def step_of(self, number, unit):
        one, two, three = self.groups[unit]
        rows = pl.ds(pl.multiple_of(one[0] * 64, 64), 64)
        inner = pl.ds(pl.multiple_of(two[0] * 16, 16), 16)
        if number == 0:
            def piece(p):
                return self.part.at[unit, pl.ds(pl.multiple_of(p * 64, 64), 64)]

            self.give(unit, 0, one, piece, lambda p: self.first.at[unit, p])
            self.first[unit, one[0]] = self.part[unit, rows, :]
        elif number == 1:
            total = self.first[unit, 0].astype(F32)
            for p in range(1, NG):
                total += self.first[unit, p].astype(F32)
            self.held[unit] = total.astype(BF)

            def piece(p):
                return self.held.at[unit, pl.ds(pl.multiple_of(p * 16, 16), 16)]

            self.give(unit, 1, two, piece, lambda p: self.second.at[unit, p])
            self.second[unit, two[0]] = self.held[unit, inner, :]
        elif number == 2:
            total = self.second[unit, 0].astype(F32)
            for p in range(1, 4):
                total += self.second[unit, p].astype(F32)
            self.third[unit, three[0]] = total.astype(BF)
            mine = self.third.at[unit, three[0]]
            self.give(unit, 2, three, lambda p: mine, lambda p: self.third.at[unit, p])
        elif number == 3:
            total = self.third[unit, 0].astype(F32)
            for p in range(1, 4):
                total += self.third[unit, p].astype(F32)
            row = pl.multiple_of(one[0] * 64 + two[0] * 16, 16)
            self.full[unit, pl.ds(row, 16), :] = total.astype(BF)

            def line(p):
                at = pl.multiple_of(one[0] * 64 + p * 16, 16)
                return self.full.at[unit, pl.ds(at, 16)]

            self.give(unit, 3, two, lambda p: line(two[0]), line)
        elif number == 4:
            def block(p):
                return self.full.at[unit, pl.ds(pl.multiple_of(p * 64, 64), 64)]

            self.give(unit, 4, one, lambda p: block(one[0]), block)

    def finish(self):
        for unit in (0, 1):
            for phase in range(5):
                wait_bytes(self.view(unit, phase), self.send.at[unit, phase])


def whole_kernel(names, *refs):
    r = types.SimpleNamespace(**dict(zip(names, refs)))
    b, g = lax.axis_index("bal"), lax.axis_index("grp")
    me = place_of(b // 4, lax.rem(b, 4), g // 2, lax.rem(b, 4) * NG + g)
    barrier = greet_all(me)
    r.loads = (
        (r.table_hbm, r.table_v), (r.w_in_hbm, r.w_in), (r.w_out_hbm, r.w_out), (r.cot_hbm, r.cot),
    )
    for k, (source, into) in enumerate(r.loads):
        pltpu.make_async_copy(source, into, r.load_sems.at[k]).start()
    rows = fetch_rows(r, me, b, g, barrier)
    early = Reduction(r, "early")
    late = Reduction(r, "late")
    z, x = b // HEADS, lax.rem(b, HEADS)
    def remote(src, dst, send, recv, at_z, at_x):
        return pltpu.make_async_remote_copy(
            src_ref=src, dst_ref=dst, send_sem=send, recv_sem=recv,
            device_id=(at_z * HEADS + at_x, g), device_id_type=MESH,
        )

    def spread(out, into, send, recv):
        for h in range(HEADS):
            @pl.when(h != x)
            def _():
                remote(out.at[h], into.at[x], send.at[h], recv.at[x], z, h).start()

            @pl.when(h == x)
            def _():
                into[h] = out[h]

    def collect(out, into, send, recv):
        for h in range(HEADS):
            @pl.when(h != x)
            def _():
                remote(out.at[h], into.at[h], send.at[h], recv.at[h], z, h).wait_recv()

    def sent(out, into, send, recv):
        for h in range(HEADS):
            @pl.when(h != x)
            def _():
                remote(out.at[h], into.at[h], send.at[h], recv.at[h], z, h).wait_send()

    embedded = r.emb[...].astype(F32)
    normed, _ = normalise(embedded)
    normed = normed.astype(BF)
    pre = dot(normed, r.w_in[...])
    sig = jax.nn.sigmoid(pre)
    act = pre * sig
    r.gate_v[...] = act[:, :HD].astype(BF)
    for h in range(HEADS):
        value, query, key = (
            act[:, part * HD + h * DH : part * HD + (h + 1) * DH] for part in (1, 2, 3)
        )
        r.kv_out[h] = jnp.concatenate([key, value], axis=1).astype(BF)
        r.q_out[h] = fold(query * 0.5).astype(BF)
    spread(r.q_out, r.q_in, r.q_send, r.q_recv)
    for dz in range(SPAN):
        for h in range(HEADS):
            @pl.when((z + dz < HEADS) & ((h != x) | (dz > 0)))
            def _():
                remote(
                    r.kv_out.at[h], r.kv_in.at[dz, x], r.kv_send.at[dz, h], r.kv_recv.at[dz, x], z + dz, h
                ).start()

            if dz == 0:
                @pl.when(h == x)
                def _():
                    r.kv_in[0, h] = r.kv_out[h]

    r.slope_v[...] = sig * (1.0 + pre * (1.0 - sig))
    r.att_v[...] = jnp.zeros_like(r.att_v)
    r.dq_v[...] = jnp.zeros_like(r.dq_v)
    places = z * HEADS * TOK + iota((HEADS * TOK, 128), 0)
    starts = r.start[:1, :]
    begin = jnp.max(jnp.where(starts <= places, starts, 0).astype(F32), axis=1, keepdims=True)
    r.begin_v[...] = jnp.broadcast_to(begin, (HEADS * TOK, 128)).astype(jnp.int32)
    collect(r.q_out, r.q_in, r.q_send, r.q_recv)
    for h in range(HEADS):
        q = unfold(r.q_in[h].astype(F32))
        r.q_v[h * TOK : (h + 1) * TOK, :] = jnp.concatenate(
            [q, jnp.zeros((TOK, DH), F32)], axis=1
        ).astype(BF)
        r.qt_v[:, h * TOK : (h + 1) * TOK] = q.T.astype(BF)

    def forward_pair(dz, i, j):
        kv = r.kv_in[dz, j]
        scores = dot_t(r.q_v[tile(i), :], kv)
        half = jnp.tanh(scores)
        more = 1.0 + half
        first = ((z - dz) * HEADS + j) * TOK
        visible = iota((TOK, TOK), 1) >= r.begin_v[tile(i), :1] - first
        if dz == 0 and i == j:
            visible &= iota((TOK, TOK), 1) <= iota((TOK, TOK), 0)
        weight = jnp.where(visible, scores * more, 0.0).astype(BF)
        r.w_v[dz, i * HEADS + j] = weight
        r.s_v[dz, i * HEADS + j] = jnp.where(
            visible, more * (1.0 + scores * (1.0 - half)), 0.0
        ).astype(BF)
        return dot(weight, kv)

    def forward(dz, i):
        keys = range(HEADS) if dz == 1 else range(i + 1) if dz == 0 else range(i, HEADS)
        total = r.att_v[tile(i), :]
        for j in keys:
            total = total + forward_pair(dz, i, j)
        r.att_v[tile(i), :] = total

    def arrived(dz):
        for h in range(HEADS):
            def arrival():
                remote(
                    r.kv_out.at[h], r.kv_in.at[dz, h], r.kv_send.at[dz, h], r.kv_recv.at[dz, h], z, h
                ).wait_recv()

            if dz == 0:
                pl.when(h != x)(arrival)
            else:
                arrival()

    for dz in range(SPAN):
        @pl.when(z >= dz)
        def _():
            arrived(dz)
            if dz == 1:
                pl.loop(0, HEADS)(functools.partial(forward, dz))
            else:
                for i in range(HEADS):
                    forward(dz, i)

    for h in range(HEADS):
        att = r.att_v[h * TOK : (h + 1) * TOK, DH:] * (2.0 / GROUP)
        r.att_out[h] = fold(att).astype(ATT)
    spread(r.att_out, r.att_in, r.a_send, r.a_recv)
    cot = r.cot[...]
    d_mixed = dot_t(cot, r.w_out[...])
    gate = r.gate_v[...].astype(F32)
    collect(r.att_out, r.att_in, r.a_send, r.a_recv)

    attended = jnp.concatenate([unfold(r.att_in[h].astype(F32)) for h in range(HEADS)], axis=1)
    level, scale = normalise(attended)
    delta = norm_grad(d_mixed * gate, level, scale)
    for h in range(HEADS):
        r.d_out[h] = fold(delta[:, h * DH : (h + 1) * DH]).astype(BF)
    spread(r.d_out, r.d_in, r.d_send, r.d_recv)
    mixed = (level * gate).astype(BF)
    r.layer_v[...] = (dot(mixed, r.w_out[...]) + r.emb[...].astype(F32)).astype(BF)
    pltpu.make_async_copy(r.layer_v, r.layer_out, r.store_sems.at[1]).start()
    d_gate = (d_mixed * level).astype(BF).astype(F32)
    r.joined[:, :HD] = (d_gate * r.slope_v[:, :HD]).astype(BF)
    embedded = r.emb[...].astype(F32)
    normed = normalise(embedded)[0].astype(BF)
    r.early_part[0] = dot_rows(normed, r.joined[:, :HD]).astype(BF)
    out_grad = dot_rows(mixed, cot)
    r.early_part[1, :HD] = out_grad[:, : WIDTH // 2].astype(BF)
    r.early_part[1, HD:] = out_grad[:, WIDTH // 2 :].astype(BF)
    early.step(0)
    collect(r.d_out, r.d_in, r.d_send, r.d_recv)
    for h in range(HEADS):
        d = unfold(r.d_in[h].astype(F32))
        r.q_v[HEADS * TOK + h * TOK : HEADS * TOK + (h + 1) * TOK, :] = jnp.concatenate(
            [jnp.zeros((TOK, DH), F32), d], axis=1
        ).astype(BF)
        r.dt_v[:, h * TOK : (h + 1) * TOK] = d.T.astype(BF)

    def backward(dz):
        def keys(j):
            kv = r.kv_in[dz, j]

            queries = range(HEADS) if dz == 1 else range(j, HEADS) if dz == 0 else range(j + 1)
            dk = dv = jnp.zeros((DH, TOK), F32)
            for i in queries:
                product = dot_t(r.q_v[tile(HEADS + i), :], kv)
                d_score = (product * r.s_v[dz, i * HEADS + j].astype(F32)).astype(BF)
                r.dq_v[tile(i), :] += dot(d_score, kv)
                dk = dk + dot(r.qt_v[:, tile(i)], d_score)
                dv = dv + dot(r.dt_v[:, tile(i)], r.w_v[dz, i * HEADS + j])
            grads = jnp.concatenate([dk, dv], axis=0) * (2.0 / GROUP)
            r.g_out[dz, j] = grads.T.astype(BF)
            if dz == 0:
                @pl.when(j != x)
                def _():
                    remote(
                        r.g_out.at[0, j], r.g_in.at[0, x], r.g_send.at[0, j], r.g_recv.at[0, x], z, j
                    ).start()

                @pl.when(j == x)
                def _():
                    r.g_in[0, j] = r.g_out[0, j]
            else:
                remote(
                    r.g_out.at[dz, j], r.g_in.at[dz, x], r.g_send.at[dz, j], r.g_recv.at[dz, x], z - dz, j
                ).start()

        if dz == 1:
            pl.loop(0, HEADS)(keys)
        else:
            for j in range(HEADS):
                keys(j)

    for dz in reversed(range(SPAN)):
        @pl.when(z >= dz)
        def _():
            backward(dz)

        early.step(SPAN - dz)

    for h in range(HEADS):
        r.dq_out[h] = fold(r.dq_v[h * TOK : (h + 1) * TOK, :DH] * (1.0 / GROUP)).astype(BF)
    spread(r.dq_out, r.dq_in, r.e_send, r.e_recv)

    spread_in, spread_scale = normalise(embedded)
    normed = spread_in.astype(BF)
    for dz in reversed(range(SPAN)):
        for h in range(HEADS):
            def arrival():
                remote(
                    r.g_out.at[dz, h], r.g_in.at[dz, h], r.g_send.at[dz, h], r.g_recv.at[dz, h], z, h
                ).wait_recv()

            if dz == 0:
                pl.when(h != x)(arrival)
            else:
                pl.when(z + dz < HEADS)(arrival)

    collect(r.dq_out, r.dq_in, r.e_send, r.e_recv)
    for h in range(HEADS):
        total = r.g_in[0, h].astype(F32)
        for dz in range(1, SPAN):
            total += jnp.where(z + dz < HEADS, r.g_in[dz, h].astype(F32), 0.0)
        r.joined[:, HD + h * DH : HD + (h + 1) * DH] = total[:, DH:].astype(BF)
        r.joined[:, 2 * HD + h * DH : 2 * HD + (h + 1) * DH] = unfold(
            r.dq_in[h].astype(F32)
        ).astype(BF)
        r.joined[:, 3 * HD + h * DH : 3 * HD + (h + 1) * DH] = total[:, :DH].astype(BF)
    r.joined[:, HD:] = (r.joined[:, HD:].astype(F32) * r.slope_v[:, HD:]).astype(BF)
    for unit in (0, 1):
        first = HD + unit * 3 * HD // 2
        block = r.joined[:, first : first + 3 * HD // 2]
        r.late_part[unit] = dot_rows(normed, block).astype(BF)
    late.step(0)
    early.step(4)
    d_normed = dot_t(r.joined[...], r.w_in[...])
    r.demb[...] = (
        norm_grad(d_normed, spread_in, spread_scale) + r.cot[...].astype(F32)
    ).astype(BF)

    def grads_of(first, count):
        return dot(hot(r.slot[:1, :] == iota((count, TOK), 0) + first), r.demb[...])

    grads = RowExchange(
        me, grads_of, r.grads_out, r.grads_in, r.sems.at[6], r.sems.at[7], r.sems.at[1]
    )
    for i in range(4):
        grads.serve(i)
        late.step(i + 1)
    early.step(5)
    pltpu.make_async_copy(r.early_full, r.early, r.store_sems.at[2]).start()
    late.step(5)
    pltpu.make_async_copy(r.late_full, r.late, r.store_sems.at[3]).start()
    grads.take()
    halves = r.grads_in[...].astype(F32).reshape(DEV, 2 * CAP, WIDTH // 2)
    gathered = jnp.concatenate([halves[:, :CAP], halves[:, CAP:]], axis=2)
    r.landed_v[...] = gathered.reshape(SLOTS, WIDTH).astype(BF)
    pltpu.make_async_copy(r.landed_v, r.landed, r.store_sems.at[4]).start()

    sent(r.q_out, r.q_in, r.q_send, r.q_recv)
    sent(r.att_out, r.att_in, r.a_send, r.a_recv)
    sent(r.d_out, r.d_in, r.d_send, r.d_recv)
    sent(r.dq_out, r.dq_in, r.e_send, r.e_recv)
    for dz in range(SPAN):
        for h in range(HEADS):
            @pl.when((z + dz < HEADS) & ((h != x) | (dz > 0)))
            def _():
                remote(
                    r.kv_out.at[h], r.kv_in.at[dz, h], r.kv_send.at[dz, h], r.kv_recv.at[dz, h], z, h
                ).wait_send()

            @pl.when((z >= dz) & ((h != x) | (dz > 0)))
            def _():
                remote(
                    r.g_out.at[dz, h], r.g_in.at[dz, h], r.g_send.at[dz, h], r.g_recv.at[dz, h], z, h
                ).wait_send()
    early.finish()
    late.finish()
    wait_bytes(r.asked.at[pl.ds(0, DEV - 1)], r.sems.at[2])
    rows.finish()
    grads.finish()
    wait_bytes(r.want_t, r.store_sems.at[0])
    wait_bytes(r.layer_v, r.store_sems.at[1])
    wait_bytes(r.early_full, r.store_sems.at[2])
    wait_bytes(r.late_full, r.store_sems.at[3])
    wait_bytes(r.landed_v, r.store_sems.at[4])


VMEM = pl.BlockSpec(memory_space=pltpu.VMEM)
ANY = pl.BlockSpec(memory_space=pl.ANY)


def whole(owner, row, seg, table, w_in, w_out, cot):
    dma = pltpu.SemaphoreType.DMA
    I32 = jnp.int32
    outs = dict(
        layer_out=((TOK, WIDTH), BF),
        want=((8, SLOTS), I32),
        landed=((SLOTS, WIDTH), BF),
        early=((2, WIDTH, HD), BF),
        late=((2, WIDTH, 3 * HD // 2), BF),
    )
    scratch = dict(
        table_v=((ROWS, WIDTH), BF),
        w_in=((WIDTH, 4 * HD), BF),
        w_out=((HD, WIDTH), BF),
        cot=((TOK, WIDTH), BF),
        emb=((TOK, WIDTH), BF),
        demb=((TOK, WIDTH), BF),
        slot=((8, TOK), I32),
        start=((8, 128), I32),
        asked=((DEV, 1, 128), I32),
        asks=((DEV, 1, 128), I32),
        want_v=((SLOTS, 128), I32),
        rows_out=((2 * SLOTS, WIDTH // 2), BF),
        rows_in=((2 * SLOTS, WIDTH // 2), BF),
        grads_out=((2 * SLOTS, WIDTH // 2), BF),
        grads_in=((2 * SLOTS, WIDTH // 2), BF),
        count_out=((8, 128), F32),
        count_in=((NB, 8, 128), F32),
        slope_v=((TOK, 4 * HD), F32),
        gate_v=((TOK, HD), BF),
        kv_out=((HEADS, TOK, 2 * DH), BF),
        q_out=((HEADS, TOK // 2, 2 * DH), BF),
        kv_in=((SPAN, HEADS, TOK, 2 * DH), BF),
        q_in=((HEADS, TOK // 2, 2 * DH), BF),
        q_v=((2 * HEADS * TOK, 2 * DH), BF),
        qt_v=((DH, HEADS * TOK), BF),
        begin_v=((HEADS * TOK, 128), I32),
        w_v=((SPAN, HEADS * HEADS, TOK, TOK), BF),
        s_v=((SPAN, HEADS * HEADS, TOK, TOK), BF),
        att_v=((HEADS * TOK, 2 * DH), F32),
        att_out=((HEADS, TOK // 2, 2 * DH), ATT),
        att_in=((HEADS, TOK // 2, 2 * DH), ATT),
        d_out=((HEADS, TOK // 2, 2 * DH), BF),
        d_in=((HEADS, TOK // 2, 2 * DH), BF),
        dt_v=((DH, HEADS * TOK), BF),
        dq_v=((HEADS * TOK, 2 * DH), F32),
        dq_out=((HEADS, TOK // 2, 2 * DH), BF),
        dq_in=((HEADS, TOK // 2, 2 * DH), BF),
        g_out=((SPAN, HEADS, TOK, 2 * DH), BF),
        g_in=((SPAN, HEADS, TOK, 2 * DH), BF),
        joined=((TOK, 4 * HD), BF),
        want_t=((8, SLOTS), I32),
        layer_v=((TOK, WIDTH), BF),
        landed_v=((SLOTS, WIDTH), BF),
    )
    for name, width in (("early", HD), ("late", 3 * HD // 2)):
        scratch |= {
            name + "_part": ((2, WIDTH, width), BF),
            name + "_held": ((2, 64, width), BF),
            name + "_first": ((2, NG, 64, width), BF),
            name + "_second": ((2, 4, 16, width), BF),
            name + "_third": ((2, 4, 16, width), BF),
            name + "_full": ((2, WIDTH, width), BF),
        }
    sems = dict(
        sems=(8,), load_sems=(4,), count_send=(NB,), count_recv=(NB,),
        kv_send=(SPAN, HEADS), kv_recv=(SPAN, HEADS), q_send=(HEADS,), q_recv=(HEADS,),
        a_send=(HEADS,), a_recv=(HEADS,), d_send=(HEADS,), d_recv=(HEADS,),
        g_send=(SPAN, HEADS), g_recv=(SPAN, HEADS), e_send=(HEADS,), e_recv=(HEADS,),
        early_send=(2, 5), early_recv=(2, 5), late_send=(2, 5), late_recv=(2, 5),
        store_sems=(5,),
    )
    names = ["owner", "row", "seg", "table_hbm", "w_in_hbm", "w_out_hbm", "cot_hbm"]
    names += [*outs, *scratch, *sems]
    return pl.pallas_call(
        functools.partial(whole_kernel, names),
        out_shape=tuple(jax.ShapeDtypeStruct(*kind) for kind in outs.values()),
        in_specs=[VMEM] * 3 + [ANY] * 4,
        out_specs=(ANY,) * len(outs),
        scratch_shapes=[pltpu.VMEM(*kind) for kind in scratch.values()]
        + [dma(shape) for shape in sems.values()],
        compiler_params=pltpu.CompilerParams(
            collective_id=0, has_side_effects=True, vmem_limit_bytes=58 << 20
        ),
        name="whole_layer",
    )(owner, row, seg, table, w_in, w_out, cot)


def finish_kernel(
    want_hbm, landed_hbm, early_hbm, late_hbm, layer_hbm,
    table_out, w_in_out, w_out_out, layer_out,
    want, landed, early, late, layer, table, w_in, w_out, load, store,
):
    pairs = [(want_hbm, want)]
    quarter = SLOTS // 4
    for k in range(4):
        rows = pl.ds(k * quarter, quarter)
        pairs.append((landed_hbm.at[rows], landed.at[rows]))
    for k in (0, 1):
        pairs.append((early_hbm.at[k], early.at[k]))
    for k in (0, 1):
        pairs.append((late_hbm.at[k], late.at[k]))
    pairs.append((layer_hbm, layer))
    loads = [pltpu.make_async_copy(*pair, load.at[k]) for k, pair in enumerate(pairs)]
    for copy in loads:
        copy.start()
    stores = []

    def put(source, into, rows):
        copy = pltpu.make_async_copy(
            source.at[rows], into.at[rows], store.at[len(stores)]
        )
        copy.start()
        stores.append(copy)

    for copy in loads[:5]:
        copy.wait()
    part = ROWS // 4
    for i in range(4):
        rows = pl.ds(i * part, part)
        chosen = hot(want[:1, :] == iota((part, SLOTS), 0) + i * part)
        table[rows, :] = dot(chosen, landed[...])
        for k in (0, 1):
            put(table, table_out, pl.ds(i * part + k * part // 2, part // 2))
        if i == 0:
            for copy in loads[5:]:
                copy.wait()
            w_in[:, :HD] = early[0].astype(F32)
            for k in (0, 1):
                left = HD + k * 3 * HD // 2
                w_in[:, left : left + 3 * HD // 2] = late[k].astype(F32)
            w_out[:, : WIDTH // 2] = early[1, :HD].astype(F32)
            w_out[:, WIDTH // 2 :] = early[1, HD:].astype(F32)
            for k in range(4):
                put(w_in, w_in_out, pl.ds(k * 128, 128))
            put(w_out, w_out_out, pl.ds(0, HD))
            put(layer, layer_out, pl.ds(0, TOK))
    for copy in stores:
        copy.wait()


def finish(*operands):
    results = (
        jax.ShapeDtypeStruct((ROWS, WIDTH), F32),
        jax.ShapeDtypeStruct((WIDTH, 4 * HD), F32),
        jax.ShapeDtypeStruct((HD, WIDTH), F32),
        jax.ShapeDtypeStruct((TOK, WIDTH), BF),
    )
    return pl.pallas_call(
        finish_kernel,
        out_shape=results,
        in_specs=[ANY] * 5,
        out_specs=(ANY,) * 4,
        scratch_shapes=[pltpu.VMEM(operand.shape, operand.dtype) for operand in operands]
        + [pltpu.VMEM(kind.shape, kind.dtype) for kind in results[:3]]
        + [pltpu.SemaphoreType.DMA((10,)), pltpu.SemaphoreType.DMA((14,))],
        compiler_params=pltpu.CompilerParams(vmem_limit_bytes=58 << 20),
        name="finish",
    )(*operands)


def per_device(table, item_owner, item_row, segment, w_in, w_out, cotangent):
    layer_out, want, landed, early, late = whole(
        item_owner.reshape(1, TOK), item_row, segment, table, w_in, w_out, cotangent[0]
    )
    table_grad, w_in_grad, w_out_grad, layer_out = finish(
        want, landed, early, late, layer_out
    )
    return (layer_out[None], table_grad, w_in_grad, w_out_grad)


def solution(mesh):
    placed = (
        P(("bal", "grp"), None),
        P("grp", "bal", None),
        P("grp", "bal"),
        P("grp", "bal"),
        P(),
        P(),
        P("grp", "bal", None),
    )
    return jax.shard_map(
        per_device,
        mesh=mesh,
        in_specs=placed,
        out_specs=(P("grp", "bal", None), P(("bal", "grp"), None), P(), P()),
        check_vma=False,
    )
```

time: 143 us -> 125 us (0.87)
  Pallas kernels: 135 us -> 125 us
  local copies, waits for them, and re-layouts: 6.33 us -> 0 us
    pallas_call x1, Pallas kernels: 130 us -> 119 us  [whole(): pl.pallas_call(functools.partial(whole_kernel, names), out_shape=tuple((j...]
    unnamed x11 -> x0, local copies, waits for them, and re-layouts: 4.86 us -> none
    squeeze x1 -> x0, local copies, waits for them, and re-layouts: 1.47 us -> none  [per_device(): item_owner[0]]
where the time goes in v4:
time: 125 us
  Pallas kernels  125 us (100%)
    pallas_call x1, Pallas kernels, whole(): pl.pallas_call(functools.partial(whole_kernel, names), out_shape=tuple((j...  119 us
    pallas_call x1, Pallas kernels, finish(): pl.pallas_call(finish_kernel, out_shape=results, in_specs=[ANY] * 5, out_...  5.88 us

profile of v4, /device:TPU:1, one launch (start us, length us, event | category | flops | bytes accessed | tf_op | source)
XLA Modules:
  0.0 125.3 jit_solution(12883372468424828681)
XLA Ops:
  0.6 118.6 %whole_layer.1 = (bf16[256,512]{1,0:T(8,128)(2,1)}, s32[8,1024]{1,0:T(8,128)}, bf16[1024,512]{1,0:T(8,128)(2,1)}, bf16[2,512,256]{2,1,0:T(8,128)(2,1)}, bf16[2,512,384]{2,1,0:T(8,128)(2,1)}) custom-call(s32[1,256]{1,0:T(1,128)} %bitcast.4, s32[1,256]{1,0:T(1,128)} %refs_1_.1, s32[1,256]{1,0:T(1,128)} %refs_2_.1, bf16[2048,512]{1,0:T(8,128)(2,1)} %refs_3_.1, ...), custom_call_target="tpu_custom_call" | custom-call | tf_op jit(solution)/shard_map/whole_layer/pallas_call | solution.py:709
  119.3 5.9 %finish.1 = (f32[2048,512]{1,0:T(8,128)}, f32[512,1024]{1,0:T(8,128)}, f32[256,512]{1,0:T(8,128)}, bf16[256,512]{1,0:T(8,128)(2,1)}) custom-call(s32[8,1024]{1,0:T(8,128)} %get-tuple-element.13.want_hbm, bf16[1024,512]{1,0:T(8,128)(2,1)} %get-tuple-element.14.landed_hbm, bf16[2,512,256]{2,1,0:T(8,128)(2,1)} %get-tuple-element.15.early_hbm, ...), custom_call_target="tpu_custom_call" | custom-call | tf_op jit(solution)/shard_map/finish/pallas_call | solution.py:783
